TPU v7x, 32 devices: a whole 2x2x4 slice. The times are simulated.
32 devices in a mesh: dp: 4 (over y, core), mp: 8 (over z, x).
Axes of the slice: x: 2, y: 2, z: 4, core: 2. Of those that a mesh axis runs over, the one named last changes fastest.
Arguments:
- block_input: bfloat16 [4096, 768], P(('dp', 'mp')), may hold values from -6 to 6
- mixer_gain: float32 [768], replicated, may hold values from 0.5 to 1.5
- in_weight: bfloat16 [768, 2304], P(None, 'mp'), may hold values from -0.21875 to 0.21875
- in_bias: float32 [2304], P('mp'), may hold values from -1.75 to 1.75
- short_taps: float32 [3, 2304], P(None, 'mp'), may hold values from -3.5 to 3.5
- skip_gain: float32 [768], P('mp'), may hold values from -6 to 6
- out_weight: bfloat16 [768, 768], P('mp'), may hold values from -0.21875 to 0.21875
- out_bias: float32 [768], replicated, may hold values from -1.75 to 1.75
- ffn_gain: float32 [768], replicated, may hold values from 0.5 to 1.5
- up_weight: bfloat16 [768, 3072], P(None, 'mp'), may hold values from -0.21875 to 0.21875
- up_bias: bfloat16 [3072], P('mp'), may hold values from -1.75 to 1.75
- down_weight: bfloat16 [3072, 768], P('mp'), may hold values from -0.109375 to 0.109375
- down_bias: float32 [768], replicated, may hold values from -1.75 to 1.75
- embed_weight: float32 [33, 64], replicated, may hold values from -6 to 6
- embed_bias: float32 [64], replicated, may hold values from -3 to 3
- embed_freq: float32 [64], replicated, may hold values from 1 to 3
- hidden_weight: float32 [64, 64], replicated, may hold values from -1.75 to 1.75
- hidden_bias: float32 [64], replicated, may hold values from -3 to 3
- hidden_freq: float32 [64], replicated, may hold values from 1 to 3
- filter_weight: float32 [64, 768], replicated, may hold values from -0.0625 to 0.0625
- decay_rate: float32 [768], replicated, may hold values from 0.5 to 3
- out_grad: bfloat16 [4096, 768], P(('dp', 'mp')), may hold values from -6 to 6
- sequence_lengths: int32 [9], replicated, may hold values from 256 to 1024, as said below
- sequence_rank: int32 [9], replicated, may hold values from 0 to 3, as said below
- sequence_offset: int32 [9], replicated, may hold values from 0 to 768, as said below
Outputs:
- block_output: bfloat16 [4096, 768], P(('dp', 'mp'))
- input_grad: float32 [4096, 768], P(('dp', 'mp'))
- penalty: float32 [], replicated
- mixer_gain_grad: float32 [768], replicated
- in_weight_grad: float32 [768, 2304], P(None, 'mp')
- in_bias_grad: float32 [2304], P('mp')
- short_taps_grad: float32 [3, 2304], P(None, 'mp')
- skip_gain_grad: float32 [768], P('mp')
- out_weight_grad: float32 [768, 768], P('mp')
- out_bias_grad: float32 [768], replicated
- ffn_gain_grad: float32 [768], replicated
- up_weight_grad: float32 [768, 3072], P(None, 'mp')
- up_bias_grad: float32 [3072], P('mp')
- down_weight_grad: float32 [3072, 768], P('mp')
- down_bias_grad: float32 [768], replicated
- embed_weight_grad: float32 [33, 64], replicated
- embed_bias_grad: float32 [64], replicated
- embed_freq_grad: float32 [64], replicated
- hidden_weight_grad: float32 [64, 64], replicated
- hidden_bias_grad: float32 [64], replicated
- hidden_freq_grad: float32 [64], replicated
- filter_weight_grad: float32 [64, 768], replicated
- decay_rate_grad: float32 [768], replicated
Inputs may be any that keep to these rules, and one draw needn't show every extreme that they name: `sequence_lengths`: 1 sequence have 1024 tokens, the others 256. `sequence_rank`: every pack holds one sequence of 1024 tokens or one to four of 256 tokens, and at least one sequence. `sequence_offset`: a multiple of 256; the sequences of one pack do not intersect and end by slot 1024; unused slots are padding.
All inputs are finite; a program needn't handle non-finite values.
Results may differ from a plain program's by a relative error of at most 0.02.
Values may be sent and summed in bfloat16 or wider, within the bound.
A program may use at most 128 MiB of HBM per device.

v0:
```python
import math

import jax
import jax.numpy as jnp
from jax import lax
from jax.sharding import PartitionSpec as P

D = 768
BANDS = 16
LONG = 1024


precise = lax.Precision.HIGHEST


def matmul_high(left, right):
    return jnp.dot(left, right, precision=precise, preferred_element_type=jnp.float32)


def matmul(left, right):
    return jnp.dot(left, right, preferred_element_type=jnp.float32)


def inner_rows(left, right):
    return lax.dot_general(
        left, right, (((0,), (0,)), ((), ())), preferred_element_type=jnp.float32
    )


def outer_cols(left, right):
    return lax.dot_general(
        left, right, (((1,), (1,)), ((), ())), preferred_element_type=jnp.float32
    )


def layer_norm(values, scaling):
    center = values - jnp.mean(values, axis=-1, keepdims=True)
    spread = jnp.mean(center * center, axis=-1, keepdims=True)
    return center * lax.rsqrt(spread + 1e-05) * scaling


def activation(values):
    return jax.nn.gelu(values, approximate=True)


def filter_values(
    embed_weight,
    embed_bias,
    embed_freq,
    hidden_weight,
    hidden_bias,
    hidden_freq,
    filter_weight,
    decay_rate,
    places,
):
    scaled = places / LONG
    harmonic = jnp.arange(1, BANDS + 1, dtype=jnp.float32)
    angles = 2.0 * math.pi * scaled[:, None] * harmonic[None, :]
    embedding = jnp.concatenate([scaled[:, None], jnp.cos(angles), jnp.sin(angles)], 1)
    first_layer = jnp.sin(embed_freq * (matmul_high(embedding, embed_weight) + embed_bias))
    second_layer = jnp.sin(hidden_freq * (matmul_high(first_layer, hidden_weight) + hidden_bias))
    kernel = matmul_high(second_layer, filter_weight) * jnp.exp(
        -scaled[:, None] * decay_rate[None, :]
    )
    penalty = jnp.sum(scaled[:, None] * kernel * kernel) / D
    return (kernel, penalty)


def long_conv(kernel, signal, segment):
    length, channel_count = signal.shape
    block_rows = min(length // 4, 128)
    block_count = length // block_rows
    kernel_major = kernel.T.astype(jnp.bfloat16)
    signal_major = signal.T.astype(jnp.bfloat16)
    kernel_edge = jnp.zeros((channel_count, block_rows), jnp.bfloat16)
    padded_kernel = jnp.concatenate([kernel_edge, kernel_major, kernel_edge], 1)
    padded_signal = jnp.concatenate(
        [jnp.zeros((channel_count, length), jnp.bfloat16), signal_major], 1
    )
    block_segment = segment.reshape(block_count, block_rows)[:, 0]
    padded_segment = jnp.concatenate([jnp.full((block_count,), -2, jnp.int32), block_segment], 0)
    row_index = jnp.arange(block_rows, dtype=jnp.int32)
    lag_table = row_index[:, None] - row_index[None, :] + block_rows

    def visit(running, lag_block):
        window = lax.dynamic_slice_in_dim(padded_kernel, lag_block * block_rows, 2 * block_rows, 1)
        toeplitz = jnp.take(window, lag_table, axis=1)
        shifted = lax.dynamic_slice_in_dim(
            padded_signal, length - lag_block * block_rows, length, 1
        ).reshape(channel_count, block_count, block_rows)
        earlier = lax.dynamic_slice_in_dim(padded_segment, block_count - lag_block, block_count, 0)
        same_block = (block_segment == earlier).astype(jnp.bfloat16)
        shifted = shifted * same_block[None, :, None]
        added = jnp.einsum("cts,cis->cit", toeplitz, shifted, preferred_element_type=jnp.float32)
        return (running + added.reshape(channel_count, length), None)

    running, _ = lax.scan(
        visit,
        jnp.zeros((channel_count, length), jnp.float32),
        jnp.arange(block_count, dtype=jnp.int32),
    )
    return running.T


def short_conv(values, taps, position):
    one_back = (
        jnp.concatenate([jnp.zeros_like(values[:1]), values[:-1]], 0)
        * (position >= 1).astype(jnp.float32)[:, None]
    )
    two_back = (
        jnp.concatenate([jnp.zeros_like(values[:2]), values[:-2]], 0)
        * (position >= 2).astype(jnp.float32)[:, None]
    )
    return taps[0] * values + taps[1] * one_back + taps[2] * two_back


def mixer(projected, taps, kernel, skip, segment, position, valid_rows):
    shortened = short_conv(projected, taps, position)
    grouped = shortened.reshape(shortened.shape[0], -1, 3)
    outer_gate = grouped[:, :, 0]
    inner_gate = grouped[:, :, 1]
    value_part = grouped[:, :, 2]
    signal = (
        (value_part * inner_gate * valid_rows[:, None]).astype(jnp.bfloat16).astype(jnp.float32)
    )
    return (long_conv(kernel, signal, segment) + skip * signal) * outer_gate


def pack_layout(lengths, owners, offsets, rank, length):
    slot_index = jnp.arange(length, dtype=jnp.int32)
    inside = (
        (owners[:, None] == rank)
        & (slot_index[None, :] >= offsets[:, None])
        & (slot_index[None, :] < offsets[:, None] + lengths[:, None])
    )
    valid_rows = jnp.any(inside, 0)
    identity = jnp.arange(lengths.shape[0], dtype=jnp.int32)
    segment = jnp.where(valid_rows, jnp.sum(jnp.where(inside, identity[:, None], 0), 0), -1)
    position = jnp.sum(jnp.where(inside, slot_index[None, :] - offsets[:, None], 0), 0)
    return (segment, position, valid_rows.astype(jnp.float32))


def per_device(
    block_input,
    mixer_gain,
    in_weight,
    in_bias,
    short_taps,
    skip_gain,
    out_weight,
    out_bias,
    ffn_gain,
    up_weight,
    up_bias,
    down_weight,
    down_bias,
    embed_weight,
    embed_bias,
    embed_freq,
    hidden_weight,
    hidden_bias,
    hidden_freq,
    filter_weight,
    decay_rate,
    out_grad,
    sequence_lengths,
    sequence_rank,
    sequence_offset,
):
    model_rank = lax.axis_index("mp")
    data_rank = lax.axis_index("dp")
    model_count = lax.axis_size("mp")
    first_rank = (data_rank == 0).astype(jnp.float32)
    segment, position, valid_rows = pack_layout(
        sequence_lengths, sequence_rank, sequence_offset, data_rank, LONG
    )
    filters = (
        embed_weight,
        embed_bias,
        embed_freq,
        hidden_weight,
        hidden_bias,
        hidden_freq,
        filter_weight,
        decay_rate,
    )
    row_values = block_input.astype(jnp.float32)
    normed, norm_back = jax.vjp(layer_norm, row_values, mixer_gain)
    gathered = lax.all_gather(normed.astype(jnp.bfloat16), "mp", axis=0, tiled=True)
    projected = matmul(gathered, in_weight) + in_bias
    slab_rows = LONG // model_count
    places = (model_rank * slab_rows + jnp.arange(slab_rows, dtype=jnp.int32)).astype(jnp.float32)

    def slab_filter(parameters):
        return filter_values(*parameters, places)

    (kernel, penalty_part), filter_back = jax.vjp(slab_filter, filters)
    kernel_low = lax.all_to_all(
        kernel.astype(jnp.bfloat16), "mp", split_axis=1, concat_axis=0, tiled=True
    )

    def mix_local(projected, taps, kernel_values, skip):
        return mixer(projected, taps, kernel_values, skip, segment, position, valid_rows)

    mixed, mixer_back = jax.vjp(
        mix_local, projected, short_taps, kernel_low.astype(jnp.float32), skip_gain
    )
    mixed_low = mixed.astype(jnp.bfloat16)
    branch = (
        lax.psum_scatter(
            matmul(mixed_low, out_weight).astype(jnp.bfloat16),
            "mp",
            scatter_dimension=0,
            tiled=True,
        ).astype(jnp.float32)
        + out_bias
    )
    middle = row_values + branch
    normed_two, ffn_norm_back = jax.vjp(layer_norm, middle, ffn_gain)
    normed_two_low = normed_two.astype(jnp.bfloat16)
    seed = out_grad.astype(jnp.float32)
    gathered_two = lax.all_gather(normed_two_low, "mp", axis=0, tiled=True)
    hidden = matmul(gathered_two, up_weight) + up_bias.astype(jnp.float32)
    active, gelu_back = jax.vjp(activation, hidden)
    active_low = active.astype(jnp.bfloat16)
    update = (
        lax.psum_scatter(
            matmul(active_low, down_weight).astype(jnp.bfloat16),
            "mp",
            scatter_dimension=0,
            tiled=True,
        ).astype(jnp.float32)
        + down_bias
    )
    received = lax.all_gather(out_grad, "mp", axis=0, tiled=True)
    weight_total = inner_rows(active_low, received)
    active_total = outer_cols(received, down_weight)
    down_weight_sum = weight_total
    hidden_grad = gelu_back(active_total)[0].astype(jnp.bfloat16)
    up_bias_sum = jnp.sum(hidden_grad.astype(jnp.float32), 0)
    up_weight_sum = inner_rows(gathered_two, hidden_grad)
    normed_two_grad = lax.psum_scatter(
        outer_cols(hidden_grad, up_weight).astype(jnp.bfloat16),
        "mp",
        scatter_dimension=0,
        tiled=True,
    ).astype(jnp.float32)
    block_output = (middle + update).astype(jnp.bfloat16)
    down_bias_part = jnp.sum(seed, 0)
    middle_norm_grad, ffn_gain_part = ffn_norm_back(normed_two_grad)
    middle_grad = seed + middle_norm_grad
    branch_grad = middle_grad.astype(jnp.bfloat16)
    out_bias_part = jnp.sum(branch_grad.astype(jnp.float32), 0)
    received = lax.all_gather(branch_grad, "mp", axis=0, tiled=True)
    weight_total = inner_rows(mixed_low, received)
    mixed_total = outer_cols(received, out_weight)
    projected_grad, taps_part, kernel_grad, skip_part = mixer_back(mixed_total)
    projected_low = projected_grad.astype(jnp.bfloat16)
    in_bias_part = jnp.sum(projected_low.astype(jnp.float32), 0)
    in_weight_part = inner_rows(gathered, projected_low)
    normed_grad = lax.psum_scatter(
        outer_cols(projected_low, in_weight).astype(jnp.bfloat16),
        "mp",
        scatter_dimension=0,
        tiled=True,
    ).astype(jnp.float32)
    input_part, mixer_gain_part = norm_back(normed_grad)
    input_grad = middle_grad + input_part
    kernel_grad_low = kernel_grad.astype(jnp.bfloat16)
    filter_seed = lax.all_to_all(
        kernel_grad_low, "mp", split_axis=0, concat_axis=1, tiled=True
    ).astype(jnp.float32)
    (filter_parts,) = filter_back((filter_seed, first_rank))
    channel_sums = (
        lax.psum(in_weight_part.astype(jnp.bfloat16), "dp").astype(jnp.float32),
        lax.psum(in_bias_part.astype(jnp.bfloat16), "dp").astype(jnp.float32),
        lax.psum(taps_part.astype(jnp.bfloat16), "dp").astype(jnp.float32),
        lax.psum(skip_part.astype(jnp.bfloat16), "dp").astype(jnp.float32),
        lax.psum(weight_total.astype(jnp.bfloat16), "dp").astype(jnp.float32),
        lax.psum(up_weight_sum.astype(jnp.bfloat16), "dp").astype(jnp.float32),
        lax.psum(up_bias_sum.astype(jnp.bfloat16), "dp").astype(jnp.float32),
        lax.psum(down_weight_sum.astype(jnp.bfloat16), "dp").astype(jnp.float32),
    )
    shared = lax.psum(
        (
            mixer_gain_part,
            ffn_gain_part,
            out_bias_part,
            down_bias_part,
            penalty_part * first_rank,
            filter_parts[0],
            filter_parts[1],
            filter_parts[2],
            filter_parts[3],
            filter_parts[4],
            filter_parts[5],
            filter_parts[6],
            filter_parts[7],
        ),
        ("dp", "mp"),
    )
    return (
        block_output,
        input_grad,
        shared[4],
        shared[0],
        channel_sums[0],
        channel_sums[1],
        channel_sums[2],
        channel_sums[3],
        channel_sums[4],
        shared[2],
        shared[1],
        channel_sums[5],
        channel_sums[6],
        channel_sums[7],
        shared[3],
        shared[5],
        shared[6],
        shared[7],
        shared[8],
        shared[9],
        shared[10],
        shared[11],
        shared[12],
    )


def solution(mesh):
    placed = (
        P(("dp", "mp"), None),
        P(),
        P(None, "mp"),
        P("mp"),
        P(None, "mp"),
        P("mp"),
        P("mp", None),
        P(),
        P(),
        P(None, "mp"),
        P("mp"),
        P("mp", None),
        P(),
        P(),
        P(),
        P(),
        P(),
        P(),
        P(),
        P(),
        P(),
        P(("dp", "mp"), None),
        P(),
        P(),
        P(),
    )
    return jax.shard_map(
        per_device,
        mesh=mesh,
        in_specs=placed,
        out_specs=(
            P(("dp", "mp"), None),
            P(("dp", "mp"), None),
            P(),
            P(),
            P(None, "mp"),
            P("mp"),
            P(None, "mp"),
            P("mp"),
            P("mp", None),
            P(),
            P(),
            P(None, "mp"),
            P("mp"),
            P("mp", None),
            P(),
            P(),
            P(),
            P(),
            P(),
            P(),
            P(),
            P(),
            P(),
        ),
        check_vma=False,
    )
```

profile of v0, /device:TPU:0, one launch (start us, length us, event | category | flops | bytes accessed | tf_op | source)
XLA Modules:
  0.0 2183.2 jit_solution(9772183377455429765)
XLA Ops:
  71.1 617.6 %while.42 = (s32[]{:T(128)}, f32[96,1024]{1,0:T(8,128)S(1)}, s32[8]{0:T(128)S(1)}, s32[8]{0:T(128)S(1)}, bf16[8,1,8,1]{2,3,1,0:T(2,128)(2,1)}, /*index=5*/bf16[8...) while((s32[]{:T(128)}, f32[96,1024]{1,0:T(8,128)S(1)}, ...), condition=%wide.region_6.7_spmd.clone.clone, body=%wide.region_5.6_spmd.clone.clone.sunk | while | flops 29229084 | bytes 25741800 | solution.py:98
  74.6 57.8 %gather_fusion = bf16[16384,96]{1,0:T(8,128)(2,1)} fusion(bf16[96,256]{0,1:T(8,128)(2,1)S(1)} %copy.154, s32[16384]{0:T(1024)S(1)} %bitcast_clamp_fusion.2), kind=kCustom, calls=%fused_computation.clone.clone.1 | custom fusion | bytes 6356992 | tf_op jit(solution)/shard_map/jvp()/while/body/eval_jaxpr/jit(_take)/gather | solution.py:88
  151.8 57.8 %gather_fusion = bf16[16384,96]{1,0:T(8,128)(2,1)} fusion(bf16[96,256]{0,1:T(8,128)(2,1)S(1)} %copy.154, s32[16384]{0:T(1024)S(1)} %bitcast_clamp_fusion.2), kind=kCustom, calls=%fused_computation.clone.clone.1 | custom fusion | bytes 6356992 | tf_op jit(solution)/shard_map/jvp()/while/body/eval_jaxpr/jit(_take)/gather | solution.py:88
  229.0 57.8 %gather_fusion = bf16[16384,96]{1,0:T(8,128)(2,1)} fusion(bf16[96,256]{0,1:T(8,128)(2,1)S(1)} %copy.154, s32[16384]{0:T(1024)S(1)} %bitcast_clamp_fusion.2), kind=kCustom, calls=%fused_computation.clone.clone.1 | custom fusion | bytes 6356992 | tf_op jit(solution)/shard_map/jvp()/while/body/eval_jaxpr/jit(_take)/gather | solution.py:88
  306.2 57.8 %gather_fusion = bf16[16384,96]{1,0:T(8,128)(2,1)} fusion(bf16[96,256]{0,1:T(8,128)(2,1)S(1)} %copy.154, s32[16384]{0:T(1024)S(1)} %bitcast_clamp_fusion.2), kind=kCustom, calls=%fused_computation.clone.clone.1 | custom fusion | bytes 6356992 | tf_op jit(solution)/shard_map/jvp()/while/body/eval_jaxpr/jit(_take)/gather | solution.py:88
  383.4 57.8 %gather_fusion = bf16[16384,96]{1,0:T(8,128)(2,1)} fusion(bf16[96,256]{0,1:T(8,128)(2,1)S(1)} %copy.154, s32[16384]{0:T(1024)S(1)} %bitcast_clamp_fusion.2), kind=kCustom, calls=%fused_computation.clone.clone.1 | custom fusion | bytes 6356992 | tf_op jit(solution)/shard_map/jvp()/while/body/eval_jaxpr/jit(_take)/gather | solution.py:88
  460.6 57.8 %gather_fusion = bf16[16384,96]{1,0:T(8,128)(2,1)} fusion(bf16[96,256]{0,1:T(8,128)(2,1)S(1)} %copy.154, s32[16384]{0:T(1024)S(1)} %bitcast_clamp_fusion.2), kind=kCustom, calls=%fused_computation.clone.clone.1 | custom fusion | bytes 6356992 | tf_op jit(solution)/shard_map/jvp()/while/body/eval_jaxpr/jit(_take)/gather | solution.py:88
  537.7 57.8 %gather_fusion = bf16[16384,96]{1,0:T(8,128)(2,1)} fusion(bf16[96,256]{0,1:T(8,128)(2,1)S(1)} %copy.154, s32[16384]{0:T(1024)S(1)} %bitcast_clamp_fusion.2), kind=kCustom, calls=%fused_computation.clone.clone.1 | custom fusion | bytes 6356992 | tf_op jit(solution)/shard_map/jvp()/while/body/eval_jaxpr/jit(_take)/gather | solution.py:88
  615.0 57.8 %gather_fusion = bf16[16384,96]{1,0:T(8,128)(2,1)} fusion(bf16[96,256]{0,1:T(8,128)(2,1)S(1)} %copy.154, s32[16384]{0:T(1024)S(1)} %bitcast_clamp_fusion.2), kind=kCustom, calls=%fused_computation.clone.clone.1 | custom fusion | bytes 6356992 | tf_op jit(solution)/shard_map/jvp()/while/body/eval_jaxpr/jit(_take)/gather | solution.py:88
  691.6 63.0 %reduce-scatter.5.cloned.1.call-done = bf16[128,768]{1,0:T(8,128)(2,1)} async-done(((bf16[1024,768]{1,0:T(8,128)(2,1)}), bf16[128,768]{1,0:T(8,128)(2,1)}) %reduce-scatter.5.cloned.1.call-update) | async-done | bytes 196624 | tf_op jit(solution)/shard_map/reduce_scatter | solution.py:211
  803.7 42.3 %all-gather.7.cloned.1.call-done = bf16[1024,768]{1,0:T(8,128)(2,1)} async-done(((bf16[128,768]{1,0:T(8,128)(2,1)}), bf16[1024,768]{1,0:T(8,128)(2,1)}) %all-gather.7.cloned.1.call-update) | async-done | bytes 1572880 | tf_op jit(solution)/shard_map/all_gather | solution.py:223
  858.5 59.8 %reduce-scatter.9.cloned.1.call-done = bf16[128,768]{1,0:T(8,128)(2,1)} async-done(((bf16[1024,768]{1,0:T(8,128)(2,1)}), bf16[128,768]{1,0:T(8,128)(2,1)}) %reduce-scatter.9.cloned.1.call-update) | async-done | bytes 196624 | tf_op jit(solution)/shard_map/reduce_scatter | solution.py:243
  919.6 65.9 %reduce-scatter.7.cloned.1.call-done = bf16[128,768]{1,0:T(8,128)(2,1)} async-done(((bf16[1024,768]{1,0:T(8,128)(2,1)}), bf16[128,768]{1,0:T(8,128)(2,1)}) %reduce-scatter.7.cloned.1.call-update) | async-done | bytes 196624 | tf_op jit(solution)/shard_map/reduce_scatter | solution.py:228
  1035.0 885.1 %while.41 = (s32[]{:T(128)}, bf16[96,1280]{0,1:T(8,128)(2,1)}, bf16[96,2048]{1,0:T(8,128)(2,1)S(1)}, s32[8]{0:T(128)S(1)}, bf16[8,96,8,128]{3,2,1,0:T(8,128)(2,1...) while((s32[]{:T(128)}, bf16[96,1280]{0,1:T(8,128)(2,1)}, ...), condition=%wide.region_16.17_spmd.clone, body=%wide.region_14.16_spmd.clone.sunk | while | flops 52477952 | bytes 24510692 | solution.py:98
  1055.5 88.3 %scatter_fusion = bf16[96,256]{0,1:T(8,128)(2,1)S(1)} fusion(bf16[96,256]{0,1:T(8,128)(2,1)S(1)} %constant_dynamic-slice_fusion.5, s32[16384]{0:T(1024)S(1)} %fusion.147, bf16[16384,96]{1,0:T(8,128)(2,1)} %bitcast.221), kind=kCustom, calls=%fused_computation.1.clone.clone.1 | custom fusion | flops 1572864 | bytes 9502720 | tf_op jit(solution)/shard_map/transpose(jvp())/while/body/eval_jaxpr/jit(_take)/scatter-add | solution.py:88
  1166.3 88.3 %scatter_fusion = bf16[96,256]{0,1:T(8,128)(2,1)S(1)} fusion(bf16[96,256]{0,1:T(8,128)(2,1)S(1)} %constant_dynamic-slice_fusion.5, s32[16384]{0:T(1024)S(1)} %fusion.147, bf16[16384,96]{1,0:T(8,128)(2,1)} %bitcast.221), kind=kCustom, calls=%fused_computation.1.clone.clone.1 | custom fusion | flops 1572864 | bytes 9502720 | tf_op jit(solution)/shard_map/transpose(jvp())/while/body/eval_jaxpr/jit(_take)/scatter-add | solution.py:88
  1277.1 88.3 %scatter_fusion = bf16[96,256]{0,1:T(8,128)(2,1)S(1)} fusion(bf16[96,256]{0,1:T(8,128)(2,1)S(1)} %constant_dynamic-slice_fusion.5, s32[16384]{0:T(1024)S(1)} %fusion.147, bf16[16384,96]{1,0:T(8,128)(2,1)} %bitcast.221), kind=kCustom, calls=%fused_computation.1.clone.clone.1 | custom fusion | flops 1572864 | bytes 9502720 | tf_op jit(solution)/shard_map/transpose(jvp())/while/body/eval_jaxpr/jit(_take)/scatter-add | solution.py:88
  1387.8 88.3 %scatter_fusion = bf16[96,256]{0,1:T(8,128)(2,1)S(1)} fusion(bf16[96,256]{0,1:T(8,128)(2,1)S(1)} %constant_dynamic-slice_fusion.5, s32[16384]{0:T(1024)S(1)} %fusion.147, bf16[16384,96]{1,0:T(8,128)(2,1)} %bitcast.221), kind=kCustom, calls=%fused_computation.1.clone.clone.1 | custom fusion | flops 1572864 | bytes 9502720 | tf_op jit(solution)/shard_map/transpose(jvp())/while/body/eval_jaxpr/jit(_take)/scatter-add | solution.py:88
  1498.4 88.3 %scatter_fusion = bf16[96,256]{0,1:T(8,128)(2,1)S(1)} fusion(bf16[96,256]{0,1:T(8,128)(2,1)S(1)} %constant_dynamic-slice_fusion.5, s32[16384]{0:T(1024)S(1)} %fusion.147, bf16[16384,96]{1,0:T(8,128)(2,1)} %bitcast.221), kind=kCustom, calls=%fused_computation.1.clone.clone.1 | custom fusion | flops 1572864 | bytes 9502720 | tf_op jit(solution)/shard_map/transpose(jvp())/while/body/eval_jaxpr/jit(_take)/scatter-add | solution.py:88
  1609.0 88.3 %scatter_fusion = bf16[96,256]{0,1:T(8,128)(2,1)S(1)} fusion(bf16[96,256]{0,1:T(8,128)(2,1)S(1)} %constant_dynamic-slice_fusion.5, s32[16384]{0:T(1024)S(1)} %fusion.147, bf16[16384,96]{1,0:T(8,128)(2,1)} %bitcast.221), kind=kCustom, calls=%fused_computation.1.clone.clone.1 | custom fusion | flops 1572864 | bytes 9502720 | tf_op jit(solution)/shard_map/transpose(jvp())/while/body/eval_jaxpr/jit(_take)/scatter-add | solution.py:88
  1719.4 88.3 %scatter_fusion = bf16[96,256]{0,1:T(8,128)(2,1)S(1)} fusion(bf16[96,256]{0,1:T(8,128)(2,1)S(1)} %constant_dynamic-slice_fusion.5, s32[16384]{0:T(1024)S(1)} %fusion.147, bf16[16384,96]{1,0:T(8,128)(2,1)} %bitcast.221), kind=kCustom, calls=%fused_computation.1.clone.clone.1 | custom fusion | flops 1572864 | bytes 9502720 | tf_op jit(solution)/shard_map/transpose(jvp())/while/body/eval_jaxpr/jit(_take)/scatter-add | solution.py:88
  1829.6 88.3 %scatter_fusion = bf16[96,256]{0,1:T(8,128)(2,1)S(1)} fusion(bf16[96,256]{0,1:T(8,128)(2,1)S(1)} %constant_dynamic-slice_fusion.5, s32[16384]{0:T(1024)S(1)} %fusion.147, bf16[16384,96]{1,0:T(8,128)(2,1)} %bitcast.221), kind=kCustom, calls=%fused_computation.1.clone.clone.1 | custom fusion | flops 1572864 | bytes 9502720 | tf_op jit(solution)/shard_map/transpose(jvp())/while/body/eval_jaxpr/jit(_take)/scatter-add | solution.py:88
  1982.6 63.2 %reduce-scatter.11.cloned.1.call-done = bf16[128,768]{1,0:T(8,128)(2,1)} async-done(((bf16[1024,768]{1,0:T(8,128)(2,1)}), bf16[128,768]{1,0:T(8,128)(2,1)}) %reduce-scatter.11.cloned.1.call-update) | async-done | bytes 196624 | tf_op jit(solution)/shard_map/reduce_scatter | solution.py:262
  2091.7 83.0 %all-reduce.18.cloned.1.call-done = f32[64,768]{1,0:T(8,128)} async-done(((f32[64,768]{1,0:T(8,128)}), f32[64,768]{1,0:T(8,128)}) %all-reduce.18.cloned.1.call-update) | async-done | bytes 196624 | tf_op jit(solution)/shard_map/psum | solution.py:285
  (527 shorter events, 604.9 us)
Async XLA Ops:
  7.2 838.8 %copy-start = (bf16[768,384]{1,0:T(8,128)(2,1)S(1)}, bf16[768,384]{1,0:T(8,128)(2,1)}, u32[]{:S(2)}) copy-start(bf16[768,384]{1,0:T(8,128)(2,1)} %param.38) | copy-start | bytes 1769476
  7.2 53.8 %all-gather.5.cloned.1.call-start = ((), (), s32[]{:S(2)}) async-start(), calls=%async_computation.6 | async-start | bytes 1769472 | tf_op jit(solution)/shard_map/all_gather | solution.py:190
  19.1 18.7 all-to-all-start
  26.3 728.2 %reduce-scatter.5.cloned.1.call-start = ((), (), s32[]{:S(2)}) async-start(), calls=%async_computation.7 | async-start | bytes 1769472 | tf_op jit(solution)/shard_map/reduce_scatter | solution.py:211
  71.0 617.8 %copy-start.11 = (bf16[1024,96]{0,1:T(8,128)(2,1)}, bf16[1024,96]{0,1:T(8,128)(2,1)S(1)}, u32[]{:S(2)}) copy-start(bf16[1024,96]{0,1:T(8,128)(2,1)S(1)} %multiply_convert_fusion.3) | copy-start | bytes 589828
  71.0 617.7 %copy-start.62 = (f32[96]{0:T(128)S(1)}, f32[96]{0:T(128)}, u32[]{:S(2)}) copy-start(f32[96]{0:T(128)} %param.34) | copy-start | bytes 1156
  71.0 617.9 %copy-start.22 = (bf16[96,768]{1,0:T(8,128)(2,1)S(1)}, bf16[96,768]{1,0:T(8,128)(2,1)}, u32[]{:S(2)}) copy-start(bf16[96,768]{1,0:T(8,128)(2,1)} %param.35) | copy-start | bytes 442372
  690.8 109.3 %copy-start.20 = (bf16[384,768]{1,0:T(8,128)(2,1)S(1)}, bf16[384,768]{1,0:T(8,128)(2,1)}, u32[]{:S(2)}) copy-start(bf16[384,768]{1,0:T(8,128)(2,1)} %param.40) | copy-start | bytes 1769476
  690.8 109.3 %all-gather.9.cloned.1.call-start = ((), (), s32[]{:S(2)}) async-start(), calls=%async_computation.10 | async-start | bytes 1769472 | tf_op jit(solution)/shard_map/all_gather | solution.py:236
  691.6 154.4 %all-gather.7.cloned.1.call-start = ((), (), s32[]{:S(2)}) async-start(), calls=%async_computation.8 | async-start | bytes 1769472 | tf_op jit(solution)/shard_map/all_gather | solution.py:223
  758.5 159.8 %reduce-scatter.9.cloned.1.call-start = ((), (), s32[]{:S(2)}) async-start(), calls=%async_computation.11 | async-start | bytes 1769472 | tf_op jit(solution)/shard_map/reduce_scatter | solution.py:243
  854.5 131.0 %reduce-scatter.7.cloned.1.call-start = ((), (), s32[]{:S(2)}) async-start(), calls=%async_computation.9 | async-start | bytes 1769472 | tf_op jit(solution)/shard_map/reduce_scatter | solution.py:228
  858.5 127.0 %copy-start.54 = (f32[768]{0:T(1024)S(1)}, f32[768]{0:T(1024)}, u32[]{:S(2)}) copy-start(f32[768]{0:T(1024)} %param.41) | copy-start | bytes 9220
  858.5 129.0 %copy-start.13 = (bf16[128,768]{1,0:T(8,128)(2,1)S(1)}, bf16[128,768]{1,0:T(8,128)(2,1)}, u32[]{:S(2)}) copy-start(bf16[128,768]{1,0:T(8,128)(2,1)} %param.50) | copy-start | bytes 589828
  858.5 131.2 %copy-start.82 = (bf16[1024,384]{1,0:T(8,128)(2,1)S(1)}, bf16[1024,384]{1,0:T(8,128)(2,1)}, u32[]{:S(2)}) copy-start(bf16[1024,384]{1,0:T(8,128)(2,1)} %copy-done.81) | copy-start | bytes 2359300
  858.5 173.6 %all-gather.11.cloned.1.call-start = ((), (), s32[]{:S(2)}) async-start(), calls=%async_computation.12 | async-start | bytes 1769472 | tf_op jit(solution)/shard_map/all_gather | solution.py:255
  988.8 988.7 %all-reduce.20.cloned.1.call-start = ((), (), s32[]{:S(2)}) async-start(), calls=%async_computation.15 | async-start | bytes 3538944 | tf_op jit(solution)/shard_map/psum | solution.py:276
  1035.0 885.1 %copy-start.10 = (f32[1024,96,1]{0,2,1:T(1,128)S(1)}, f32[1024,96,1]{0,2,1:T(1,128)}, u32[]{:S(2)}) copy-start(f32[1024,96,1]{0,2,1:T(1,128)} %copy-done.9) | copy-start | bytes 1179652
  1035.0 885.1 %copy-start.31 = (f32[1024]{0:T(1024)S(1)}, f32[1024]{0:T(1024)}, u32[]{:S(2)}) copy-start(f32[1024]{0:T(1024)} %copy-done.30) | copy-start | bytes 12292
  1035.0 885.1 %copy-start.63 = (f32[96]{0:T(128)S(1)}, f32[96]{0:T(128)}, u32[]{:S(2)}) copy-start(f32[96]{0:T(128)} %param.34) | copy-start | bytes 1156
  1931.7 114.2 %reduce-scatter.11.cloned.1.call-start = ((), (), s32[]{:S(2)}) async-start(), calls=%async_computation.13 | async-start | bytes 1769472 | tf_op jit(solution)/shard_map/reduce_scatter | solution.py:262
  1935.8 14.5 all-to-all-start.1
  1939.4 235.3 %all-reduce.18.cloned.1.call-start = ((), (), s32[]{:S(2)}) async-start(), calls=%async_computation.14 | async-start | bytes 393216 | tf_op jit(solution)/shard_map/psum | solution.py:285
  1981.9 194.5 %copy-start.1 = (bf16[768,384]{1,0:T(8,128)(2,1)S(1)}, bf16[768,384]{1,0:T(8,128)(2,1)}, u32[]{:S(2)}) copy-start(bf16[768,384]{1,0:T(8,128)(2,1)} %param.38) | copy-start | bytes 1769476
  (72 other events, 1422.7 us)
Sparse Core Ops, SparseCore 0:
  12.0 48.9 all-gather.4
  690.9 63.6 reduce-scatter.4
  757.0 43.0 all-gather.8
  802.9 42.9 all-gather.6
  854.7 63.6 reduce-scatter.8
  921.6 63.8 reduce-scatter.6
  989.0 43.0 all-gather.10
  1931.8 45.6 all-reduce.19
  1981.0 64.8 reduce-scatter.10
  2052.8 121.9 all-reduce.17
where the time goes:
time: 2190 us; the launch traced here: 2180 us
  other arithmetic  797 us (36%)
  local copies, waits for them, and re-layouts  663 us (30%)
  waiting for transfers between devices  512 us (23%)
  matrix products  118 us (5%)
  blocking collectives  48.9 us (2%)
    scatter-add x8, other arithmetic, visit(): toeplitz = jnp.take(window, lag_table, axis=1)  706 us
    gather x16, local copies, waits for them, and re-layouts, visit(): toeplitz = jnp.take(window, lag_table, axis=1)  513 us
    psum x1, waiting for transfers between devices, per_device(): lax.psum((mixer_gain_part, ffn_gain_part, out_bias_part, down_bias_part,...  83 us
    dot_general x24, matrix products, visit(): jnp.einsum('cts,cis->cit', toeplitz, shifted, preferred_element_type=jnp....  80 us
    reduce_scatter x1, waiting for transfers between devices, per_device(): lax.psum_scatter(matmul(active_low, down_weight).astype(jnp.bfloat16), 'm...  65.9 us
    reduce_scatter x1, waiting for transfers between devices, per_device(): lax.psum_scatter(outer_cols(projected_low, in_weight).astype(jnp.bfloat16...  63.2 us
    reduce_scatter x1, waiting for transfers between devices, per_device(): lax.psum_scatter(matmul(mixed_low, out_weight).astype(jnp.bfloat16), 'mp'...  63 us
    reduce_scatter x1, waiting for transfers between devices, per_device(): lax.psum_scatter(outer_cols(hidden_grad, up_weight).astype(jnp.bfloat16),...  59.8 us
  transfers between devices with their start and end apart: 12, of which 11 were waited for; matrix products, arithmetic and copies ran while one was open for 2% of the time, Pallas kernels for 0%

commit v1 on v0

--- a/solution.py
+++ b/solution.py
@@ -2,6 +2,7 @@
 
 import jax
 import jax.numpy as jnp
+import numpy as np
 from jax import lax
 from jax.sharding import PartitionSpec as P
 
@@ -67,40 +68,95 @@
     return (kernel, penalty)
 
 
-def long_conv(kernel, signal, segment):
-    length, channel_count = signal.shape
-    block_rows = min(length // 4, 128)
-    block_count = length // block_rows
-    kernel_major = kernel.T.astype(jnp.bfloat16)
-    signal_major = signal.T.astype(jnp.bfloat16)
-    kernel_edge = jnp.zeros((channel_count, block_rows), jnp.bfloat16)
-    padded_kernel = jnp.concatenate([kernel_edge, kernel_major, kernel_edge], 1)
-    padded_signal = jnp.concatenate(
-        [jnp.zeros((channel_count, length), jnp.bfloat16), signal_major], 1
-    )
-    block_segment = segment.reshape(block_count, block_rows)[:, 0]
-    padded_segment = jnp.concatenate([jnp.full((block_count,), -2, jnp.int32), block_segment], 0)
-    row_index = jnp.arange(block_rows, dtype=jnp.int32)
-    lag_table = row_index[:, None] - row_index[None, :] + block_rows
-
-    def visit(running, lag_block):
-        window = lax.dynamic_slice_in_dim(padded_kernel, lag_block * block_rows, 2 * block_rows, 1)
-        toeplitz = jnp.take(window, lag_table, axis=1)
-        shifted = lax.dynamic_slice_in_dim(
-            padded_signal, length - lag_block * block_rows, length, 1
-        ).reshape(channel_count, block_count, block_rows)
-        earlier = lax.dynamic_slice_in_dim(padded_segment, block_count - lag_block, block_count, 0)
-        same_block = (block_segment == earlier).astype(jnp.bfloat16)
-        shifted = shifted * same_block[None, :, None]
-        added = jnp.einsum("cts,cis->cit", toeplitz, shifted, preferred_element_type=jnp.float32)
-        return (running + added.reshape(channel_count, length), None)
-
-    running, _ = lax.scan(
-        visit,
-        jnp.zeros((channel_count, length), jnp.float32),
-        jnp.arange(block_count, dtype=jnp.int32),
-    )
-    return running.T
+BLOCK = 256
+BINS = 2 * BLOCK
+
+
+def wave_table(shift):
+    bins = np.arange(BLOCK)[:, None]
+    angle = np.pi * (2 * bins + 1) * (np.arange(BLOCK)[None, :] + shift) / BINS
+    return np.concatenate([np.cos(angle), -np.sin(angle)], 0)
+
+
+NEAR = wave_table(0)
+FAR = wave_table(-BLOCK)
+
+
+def low_dot(left, right):
+    return jnp.dot(
+        jnp.asarray(left, jnp.bfloat16),
+        right.astype(jnp.bfloat16),
+        preferred_element_type=jnp.float32,
+    )
+
+
+def times(left, right):
+    lr, li, rr, ri = left[:BLOCK], left[BLOCK:], right[:BLOCK], right[BLOCK:]
+    return jnp.concatenate([lr * rr - li * ri, lr * ri + li * rr], 0)
+
+
+def times_conj(left, right):
+    lr, li, rr, ri = left[:BLOCK], left[BLOCK:], right[:BLOCK], right[BLOCK:]
+    return jnp.concatenate([lr * rr + li * ri, lr * ri - li * rr], 0)
+
+
+def blocks_of(values):
+    return [values[i : i + BLOCK] for i in range(0, values.shape[0], BLOCK)]
+
+
+def kernel_spectra(kernel):
+    parts = blocks_of(kernel)
+    first = [low_dot(NEAR, parts[0])]
+    return first + [
+        low_dot(np.concatenate([NEAR, FAR], 1), jnp.concatenate([now, before], 0))
+        for now, before in zip(parts[1:], parts[:-1])
+    ]
+
+
+@jax.custom_vjp
+def long_conv(kernel, signal, joined):
+    return long_conv_keep(kernel, signal, joined)[0]
+
+
+def long_conv_keep(kernel, signal, joined):
+    spectra = kernel_spectra(kernel)
+    waves = [low_dot(NEAR, part) for part in blocks_of(signal)]
+    out = []
+    for i in range(len(waves)):
+        total = sum(joined[i, p] * times(spectra[i - p], waves[p]) for p in range(i + 1))
+        out.append(low_dot(NEAR.T / BLOCK, total))
+    return jnp.concatenate(out, 0), (spectra, waves, joined)
+
+
+def long_conv_back(kept, grad):
+    spectra, waves, joined = kept
+    count = len(waves)
+    back = [low_dot(NEAR, part) for part in blocks_of(grad)]
+    signal_grad = []
+    for p in range(count):
+        total = sum(
+            joined[i, p] * times_conj(spectra[i - p], back[i]) for i in range(p, count)
+        )
+        signal_grad.append(low_dot(NEAR.T / BLOCK, total))
+    spectra_grad = []
+    for d in range(count):
+        spectra_grad.append(
+            sum(joined[i, i - d] * times_conj(waves[i - d], back[i]) for i in range(d, count))
+        )
+    kernel_grad = []
+    for d in range(count):
+        part = low_dot(NEAR.T / BLOCK, spectra_grad[d])
+        if d + 1 < count:
+            part = part + low_dot(FAR.T / BLOCK, spectra_grad[d + 1])
+        kernel_grad.append(part)
+    return (
+        jnp.concatenate(kernel_grad, 0),
+        jnp.concatenate(signal_grad, 0),
+        jnp.zeros_like(joined),
+    )
+
+
+long_conv.defvjp(long_conv_keep, long_conv_back)
 
 
 def short_conv(values, taps, position):
@@ -124,7 +180,11 @@
     signal = (
         (value_part * inner_gate * valid_rows[:, None]).astype(jnp.bfloat16).astype(jnp.float32)
     )
-    return (long_conv(kernel, signal, segment) + skip * signal) * outer_gate
+    block_segment = segment[::BLOCK]
+    joined = (
+        (block_segment[:, None] == block_segment[None, :]) & (block_segment >= 0)[:, None]
+    ).astype(jnp.float32)
+    return (long_conv(kernel, signal, joined) + skip * signal) * outer_gate
 
 
 def pack_layout(lengths, owners, offsets, rank, length):
@@ -189,16 +249,19 @@
     normed, norm_back = jax.vjp(layer_norm, row_values, mixer_gain)
     gathered = lax.all_gather(normed.astype(jnp.bfloat16), "mp", axis=0, tiled=True)
     projected = matmul(gathered, in_weight) + in_bias
-    slab_rows = LONG // model_count
-    places = (model_rank * slab_rows + jnp.arange(slab_rows, dtype=jnp.int32)).astype(jnp.float32)
-
-    def slab_filter(parameters):
+    channel_count = in_weight.shape[1] // 3
+    places = jnp.arange(LONG, dtype=jnp.float32)
+    own_channels = model_rank * channel_count
+    local_filters = filters[:6] + (
+        lax.dynamic_slice_in_dim(filter_weight, own_channels, channel_count, 1),
+        lax.dynamic_slice_in_dim(decay_rate, own_channels, channel_count, 0),
+    )
+
+    def own_filter(parameters):
         return filter_values(*parameters, places)
 
-    (kernel, penalty_part), filter_back = jax.vjp(slab_filter, filters)
-    kernel_low = lax.all_to_all(
-        kernel.astype(jnp.bfloat16), "mp", split_axis=1, concat_axis=0, tiled=True
-    )
+    (kernel, penalty_part), filter_back = jax.vjp(own_filter, local_filters)
+    kernel_low = kernel.astype(jnp.bfloat16)
 
     def mix_local(projected, taps, kernel_values, skip):
         return mixer(projected, taps, kernel_values, skip, segment, position, valid_rows)
@@ -267,11 +330,7 @@
     ).astype(jnp.float32)
     input_part, mixer_gain_part = norm_back(normed_grad)
     input_grad = middle_grad + input_part
-    kernel_grad_low = kernel_grad.astype(jnp.bfloat16)
-    filter_seed = lax.all_to_all(
-        kernel_grad_low, "mp", split_axis=0, concat_axis=1, tiled=True
-    ).astype(jnp.float32)
-    (filter_parts,) = filter_back((filter_seed, first_rank))
+    (filter_parts,) = filter_back((kernel_grad, first_rank))
     channel_sums = (
         lax.psum(in_weight_part.astype(jnp.bfloat16), "dp").astype(jnp.float32),
         lax.psum(in_bias_part.astype(jnp.bfloat16), "dp").astype(jnp.float32),
@@ -295,11 +354,13 @@
             filter_parts[3],
             filter_parts[4],
             filter_parts[5],
-            filter_parts[6],
-            filter_parts[7],
         ),
         ("dp", "mp"),
     )
+    filter_weight_grad = lax.all_gather(
+        lax.psum(filter_parts[6], "dp"), "mp", axis=1, tiled=True
+    )
+    decay_grad = lax.all_gather(lax.psum(filter_parts[7], "dp"), "mp", axis=0, tiled=True)
     return (
         block_output,
         input_grad,
@@ -322,8 +383,8 @@
         shared[8],
         shared[9],
         shared[10],
-        shared[11],
-        shared[12],
+        filter_weight_grad,
+        decay_grad,
     )
 
 

time: 2190 us -> 620 us (0.28)
  other arithmetic: 797 us -> 50.6 us
  local copies, waits for them, and re-layouts: 663 us -> 24.3 us
  waiting for transfers between devices: 512 us -> 343 us
  blocking collectives: 48.9 us -> 111 us
  matrix products: 118 us -> 71.7 us
    scatter-add x8 -> x0, other arithmetic: 706 us -> none  [visit(): toeplitz = jnp.take(window, lag_table, axis=1)]
    gather x16 -> x0, local copies, waits for them, and re-layouts: 513 us -> none  [visit(): toeplitz = jnp.take(window, lag_table, axis=1)]
    psum x1 -> x0, waiting for transfers between devices: 83 us -> none  [per_device(): lax.psum((mixer_gain_part, ffn_gain_part, out_bias_part, down_bias_part,...]
    reduce_scatter x1, waiting for transfers between devices: 63.2 us -> 4.77 us  [per_device(): lax.psum_scatter(outer_cols(projected_low, in_weight).astype(jnp.bfloat16...]
    dynamic_update_slice x32 -> x0, other arithmetic: 55.6 us -> none  [the longest x24 49.5 us: long_conv(): lax.scan(visit, jnp.zeros((channel_count, length), jnp.float32), jnp.aran...]
    convert_element_type x11 -> x0, local copies, waits for them, and re-layouts: 55.6 us -> none  [the longest x8 54.6 us: visit(): jnp.einsum('cts,cis->cit', toeplitz, shifted, preferred_element_type=jnp....]
    dot_general x24 -> x30, matrix products: 80 us -> 26.2 us  [the longest x15 16.5 us: mixer(): return (long_conv(kernel, signal, joined) + skip * signal) * outer_gate]
    add_any x16 -> x0, local copies, waits for them, and re-layouts: 39.2 us -> none  [the longest x8 21.3 us: visit(): lax.dynamic_slice_in_dim(padded_signal, length - lag_block * block_rows,...]
  transfers between devices with their start and end apart: 12 -> 9, of which waited for: 11 -> 8; matrix products, arithmetic and copies ran while one was open for 2% -> 12% of each run, Pallas kernels for 0% -> 0%
where the time goes in v1:
time: 620 us; the launch traced here: 618 us
  waiting for transfers between devices  343 us (55%)
  blocking collectives  111 us (18%)
  matrix products  71.7 us (12%)
  other arithmetic  50.6 us (8%)
  local copies, waits for them, and re-layouts  24.3 us (4%)
  between operations  16.8 us (3%)
    reduce_scatter x1, waiting for transfers between devices, per_device(): lax.psum_scatter(matmul(active_low, down_weight).astype(jnp.bfloat16), 'm...  64.1 us
    reduce_scatter x1, waiting for transfers between devices, per_device(): lax.psum_scatter(matmul(mixed_low, out_weight).astype(jnp.bfloat16), 'mp'...  63.1 us
    reduce_scatter x1, waiting for transfers between devices, per_device(): lax.psum_scatter(outer_cols(hidden_grad, up_weight).astype(jnp.bfloat16),...  59.7 us
    all_gather x1, waiting for transfers between devices, per_device(): gathered_two = lax.all_gather(normed_two_low, 'mp', axis=0, tiled=True)  42.1 us
    psum x1, blocking collectives, per_device(): lax.psum((mixer_gain_part, ffn_gain_part, out_bias_part, down_bias_part,...  41.4 us
    all_gather x1, waiting for transfers between devices, per_device(): received = lax.all_gather(out_grad, 'mp', axis=0, tiled=True)  41.3 us
    all_gather x1, waiting for transfers between devices, per_device(): received = lax.all_gather(branch_grad, 'mp', axis=0, tiled=True)  34 us
    all_gather x1, waiting for transfers between devices, per_device(): lax.all_gather(normed.astype(jnp.bfloat16), 'mp', axis=0, tiled=True)  33.2 us
  transfers between devices with their start and end apart: 9, of which 8 were waited for; matrix products, arithmetic and copies ran while one was open for 12% of the time, Pallas kernels for 0%

profile of v1, /device:TPU:0, one launch (start us, length us, event | category | flops | bytes accessed | tf_op | source)
XLA Modules:
  0.0 617.7 jit_solution(3103330388032570234)
XLA Ops:
  20.4 3.1 fusion.37
  25.1 33.2 %all-gather.6.cloned.1.call-done = bf16[1024,768]{1,0:T(8,128)(2,1)} async-done(((bf16[128,768]{1,0:T(8,128)(2,1)}), bf16[1024,768]{1,0:T(8,128)(2,1)}) %all-gather.6.cloned.1.call-update) | async-done | bytes 1572880 | tf_op jit(solution)/shard_map/all_gather | solution.py:250
  64.8 3.7 fusion.159
  76.4 2.8 fusion.103
  83.3 63.1 %reduce-scatter.5.cloned.1.call-done = bf16[128,768]{1,0:T(8,128)(2,1)} async-done(((bf16[1024,768]{1,0:T(8,128)(2,1)}), bf16[128,768]{1,0:T(8,128)(2,1)}) %reduce-scatter.5.cloned.1.call-update) | async-done | bytes 196624 | tf_op jit(solution)/shard_map/reduce_scatter | solution.py:274
  150.7 41.3 %all-gather.10.cloned.1.call-done = bf16[1024,768]{1,0:T(8,128)(2,1)} async-done(((bf16[128,768]{1,0:T(8,128)(2,1)}), bf16[1024,768]{1,0:T(8,128)(2,1)}) %all-gather.10.cloned.1.call-update) | async-done | bytes 1572880 | tf_op jit(solution)/shard_map/all_gather | solution.py:299
  191.9 3.7 fusion.161
  195.7 42.1 %all-gather.8.cloned.1.call-done = bf16[1024,768]{1,0:T(8,128)(2,1)} async-done(((bf16[128,768]{1,0:T(8,128)(2,1)}), bf16[1024,768]{1,0:T(8,128)(2,1)}) %all-gather.8.cloned.1.call-update) | async-done | bytes 1572880 | tf_op jit(solution)/shard_map/all_gather | solution.py:286
  237.8 5.6 fusion.153
  246.5 4.0 convolution_convert_fusion.2
  250.5 59.7 %reduce-scatter.9.cloned.1.call-done = bf16[128,768]{1,0:T(8,128)(2,1)} async-done(((bf16[1024,768]{1,0:T(8,128)(2,1)}), bf16[128,768]{1,0:T(8,128)(2,1)}) %reduce-scatter.9.cloned.1.call-update) | async-done | bytes 196624 | tf_op jit(solution)/shard_map/reduce_scatter | solution.py:306
  313.2 64.1 %reduce-scatter.7.cloned.1.call-done = bf16[128,768]{1,0:T(8,128)(2,1)} async-done(((bf16[1024,768]{1,0:T(8,128)(2,1)}), bf16[128,768]{1,0:T(8,128)(2,1)}) %reduce-scatter.7.cloned.1.call-update) | async-done | bytes 196624 | tf_op jit(solution)/shard_map/reduce_scatter | solution.py:291
  386.3 3.6 convolution_convert_fusion.5
  391.7 34.0 %all-gather.12.cloned.1.call-done = bf16[1024,768]{1,0:T(8,128)(2,1)} async-done(((bf16[128,768]{1,0:T(8,128)(2,1)}), bf16[1024,768]{1,0:T(8,128)(2,1)}) %all-gather.12.cloned.1.call-update) | async-done | bytes 1572880 | tf_op jit(solution)/shard_map/all_gather | solution.py:318
  438.0 2.9 fusion.101
  451.2 2.5 fusion.130
  458.8 2.5 fusion.78
  461.3 4.0 fusion.99
  474.0 12.0 %all-reduce.12 = (f32[64,96]{1,0:T(8,128)S(1)}, f32[96]{0:T(128)}) all-reduce(f32[64,96]{1,0:T(8,128)S(1)} %fusion.46, f32[96]{0:T(128)S(1)} %get-tuple-element.28), channel_id=1, replica_groups=mesh['dp'=4,'mp'=8] {'dp'}, use_global_device_ids=true, to_apply=%region_49.50 | all-reduce | flops 6240 | bytes 49920 | tf_op jit(solution)/shard_map/psum | solution.py:361
  485.9 31.2 %all-gather = f32[8,96,64]{1,2,0:T(8,128)S(1)} all-gather(f32[1,96,64]{1,2,0:T(8,128)S(1)} %bitcast.132), channel_id=1, replica_groups=mesh['dp'=4,'mp'=8] {'mp'}, dimensions={0}, use_global_device_ids=true | all-gather | bytes 221184 | tf_op jit(solution)/shard_map/all_gather | solution.py:360
  519.1 6.1 all-reduce.13
  528.4 20.1 %all-reduce.10 = f32[768]{0:T(1024)} all-reduce(f32[768]{0:T(1024)S(1)} %dynamic-update-slice), channel_id=1, replica_groups=mesh['dp'=4,'mp'=8] {'mp'}, use_global_device_ids=true, to_apply=%add.10 | all-reduce | flops 768 | bytes 6144
  560.7 4.8 reduce-scatter.11.cloned.1.call-done
  569.8 41.4 %all-reduce.11 = (f32[]{:T(128)}, f32[768]{0:T(1024)}, f32[768]{0:T(1024)}, f32[768]{0:T(1024)}, f32[768]{0:T(1024)}, /*index=5*/f32[33,64]{1,0:T(8,128)}, f32[6...) all-reduce(f32[]{:T(128)S(6)} %mul.1114, ...), channel_id=1, replica_groups=mesh['dp'=4,'mp'=8] {'dp','mp'}, use_global_device_ids=true, to_apply=%region_16.17 | all-reduce | flops 9537 | bytes 76296 | tf_op jit(solution)/shard_map/psum | solution.py:344
  (377 shorter events, 109.4 us)
Async XLA Ops:
  7.2 230.6 %copy-start = (bf16[768,384]{1,0:T(8,128)(2,1)S(1)}, bf16[768,384]{1,0:T(8,128)(2,1)}, u32[]{:S(2)}) copy-start(bf16[768,384]{1,0:T(8,128)(2,1)} %param.61) | copy-start | bytes 1769476
  7.3 51.0 %all-gather.6.cloned.1.call-start = ((), (), s32[]{:S(2)}) async-start(), calls=%async_computation.4 | async-start | bytes 1769472 | tf_op jit(solution)/shard_map/all_gather | solution.py:250
  11.4 135.0 %reduce-scatter.5.cloned.1.call-start = ((), (), s32[]{:S(2)}) async-start(), calls=%async_computation.5 | async-start | bytes 1769472 | tf_op jit(solution)/shard_map/reduce_scatter | solution.py:274
  16.9 43.6 %copy-start.76 = (f32[288]{0:T(512)}, f32[288]{0:T(512)S(1)}, u32[]{:S(2)}) copy-start(f32[288]{0:T(512)S(1)} %get-tuple-element.36) | copy-start | bytes 3460
  16.9 43.6 %copy-start.78 = (f32[288]{0:T(512)}, f32[288]{0:T(512)S(1)}, u32[]{:S(2)}) copy-start(f32[288]{0:T(512)S(1)} %get-tuple-element.37) | copy-start | bytes 3460
  24.6 46.4 %copy-start.12 = (f32[512,96]{0,1:T(8,128)}, f32[512,96]{0,1:T(8,128)S(1)}, u32[]{:S(2)}) copy-start(f32[512,96]{0,1:T(8,128)S(1)} %fusion.10) | copy-start | bytes 589828
  25.1 45.9 %copy-start.37 = (f32[512,96]{0,1:T(8,128)}, f32[512,96]{0,1:T(8,128)S(1)}, u32[]{:S(2)}) copy-start(f32[512,96]{0,1:T(8,128)S(1)} %fusion.9) | copy-start | bytes 589828
  69.7 361.6 %copy-start.5 = (f32[512,96]{0,1:T(8,128)}, f32[512,96]{0,1:T(8,128)S(1)}, u32[]{:S(2)}) copy-start(f32[512,96]{0,1:T(8,128)S(1)} %fusion.121) | copy-start | bytes 589828
  69.9 360.5 %copy-start.7 = (f32[512,96]{0,1:T(8,128)}, f32[512,96]{0,1:T(8,128)S(1)}, u32[]{:S(2)}) copy-start(f32[512,96]{0,1:T(8,128)S(1)} %fusion.123) | copy-start | bytes 589828
  80.8 65.7 %copy-start.3 = (bf16[128,768]{1,0:T(8,128)(2,1)S(1)}, bf16[128,768]{1,0:T(8,128)(2,1)}, u32[]{:S(2)}) copy-start(bf16[128,768]{1,0:T(8,128)(2,1)} %param.52) | copy-start | bytes 589828
  80.8 65.7 %copy-start.69 = (f32[768]{0:T(1024)S(1)}, f32[768]{0:T(1024)}, u32[]{:S(2)}) copy-start(f32[768]{0:T(1024)} %param.59) | copy-start | bytes 9220
  82.5 66.1 %copy-start.71 = (f32[768]{0:T(1024)S(1)}, f32[768]{0:T(1024)}, u32[]{:S(2)}) copy-start(f32[768]{0:T(1024)} %param.60) | copy-start | bytes 9220
  82.5 68.1 %copy-start.103 = (bf16[384]{0:T(512)(128)(2,1)S(1)}, bf16[384]{0:T(512)(128)(2,1)}, u32[]{:S(2)}) copy-start(bf16[384]{0:T(512)(128)(2,1)} %param.62) | copy-start | bytes 2308
  82.5 109.4 %all-gather.10.cloned.1.call-start = ((), (), s32[]{:S(2)}) async-start(), calls=%async_computation.8 | async-start | bytes 1769472 | tf_op jit(solution)/shard_map/all_gather | solution.py:299
  83.3 154.5 %all-gather.8.cloned.1.call-start = ((), (), s32[]{:S(2)}) async-start(), calls=%async_computation.6 | async-start | bytes 1769472 | tf_op jit(solution)/shard_map/all_gather | solution.py:286
  147.5 48.2 %copy-start.91 = (f32[128]{0:T(128)}, f32[128]{0:T(128)S(1)}, u32[]{:S(2)}) copy-start(f32[128]{0:T(128)S(1)} %broadcast_multiply_fusion) | copy-start | bytes 1540
  148.6 47.0 %copy-start.106 = (f32[128]{0:T(128)}, f32[128]{0:T(128)S(1)}, u32[]{:S(2)}) copy-start(f32[128]{0:T(128)S(1)} %multiply_reduce_fusion.4) | copy-start | bytes 1540
  148.7 47.0 %copy-start.98 = (f32[128]{0:T(128)}, f32[128]{0:T(128)S(1)}, u32[]{:S(2)}) copy-start(f32[128]{0:T(128)S(1)} %fusion.138) | copy-start | bytes 1540
  150.4 159.8 %reduce-scatter.9.cloned.1.call-start = ((), (), s32[]{:S(2)}) async-start(), calls=%async_computation.9 | async-start | bytes 1769472 | tf_op jit(solution)/shard_map/reduce_scatter | solution.py:306
  246.4 130.9 %reduce-scatter.7.cloned.1.call-start = ((), (), s32[]{:S(2)}) async-start(), calls=%async_computation.7 | async-start | bytes 1769472 | tf_op jit(solution)/shard_map/reduce_scatter | solution.py:291
  250.5 59.8 %copy-start.11 = (bf16[128,768]{1,0:T(8,128)(2,1)S(1)}, bf16[128,768]{1,0:T(8,128)(2,1)}, u32[]{:S(2)}) copy-start(bf16[128,768]{1,0:T(8,128)(2,1)} %reduce-scatter.5.cloned.1.call-done) | copy-start | bytes 589828
  250.5 175.2 %all-gather.12.cloned.1.call-start = ((), (), s32[]{:S(2)}) async-start(), calls=%async_computation.10 | async-start | bytes 1769472 | tf_op jit(solution)/shard_map/all_gather | solution.py:318
  382.4 172.2 %all-reduce.17.cloned.1.call-start = ((), (), s32[]{:S(2)}) async-start(), calls=%async_computation.12 | async-start | bytes 3538944 | tf_op jit(solution)/shard_map/psum | solution.py:335
  451.1 114.4 %reduce-scatter.11.cloned.1.call-start = ((), (), s32[]{:S(2)}) async-start(), calls=%async_computation.11 | async-start | bytes 1769472 | tf_op jit(solution)/shard_map/reduce_scatter | solution.py:325
  (98 other events, 829.0 us)
Sparse Core Ops, SparseCore 0:
  11.5 46.7 all-gather.5
  82.7 63.7 reduce-scatter.4
  148.8 43.0 all-gather.9
  194.8 42.9 all-gather.7
  246.6 63.6 reduce-scatter.8
  313.5 63.8 reduce-scatter.6
  382.5 43.1 all-gather.11
  451.2 45.8 all-reduce.16
  500.5 64.8 reduce-scatter.10

commit v2 on v0

v2 whole, which is shorter than its diff:
```python
import functools
import math
import types

import jax
import jax.numpy as jnp
import numpy as np
from jax import lax
from jax.experimental import pallas as pl
from jax.experimental.pallas import tpu as pltpu
from jax.sharding import PartitionSpec as P

D = 768
BANDS = 16
EMB = 2 * BANDS + 1
FILT = 64
LONG = 1024
BLOCK = 256
BINS = 2 * BLOCK
COUNT = LONG // BLOCK
LANES = 128
WIDE = 3 * LANES
MESH = pl.DeviceIdType.MESH
BF16 = jnp.bfloat16
F32 = jnp.float32
EPS = 1e-05
ROOT = math.sqrt(2.0 / math.pi)
CUBE = 0.044715

PAY_VEC, PAY_PEN, PAY_HID, PAY_EMB, PAY_ROWS = 0, 18, 24, 88, 128
SHARD_DECAY, SHARD_PAR, SHARD_ROWS = 64, 72, 96


def wave_table(shift):
    bins = np.arange(BLOCK)[:, None]
    angle = np.pi * (2 * bins + 1) * (np.arange(BLOCK)[None, :] + shift) / BINS
    return np.concatenate([np.cos(angle), -np.sin(angle)], 0)


NEAR, FAR = wave_table(0), wave_table(-BLOCK)
WAVES = np.concatenate([NEAR, FAR], 1)
UNWAVES = np.concatenate([NEAR.T, FAR.T], 1) / BLOCK


def position_features():
    tau = np.arange(LONG) / LONG
    angles = 2.0 * np.pi * np.arange(1, BANDS + 1)[:, None] * tau[None, :]
    return np.concatenate([tau[None, :], np.cos(angles), np.sin(angles)], 0)


def dot(left, right, dims=((1,), (0,)), precision=None):
    return lax.dot_general(
        left, right, (dims, ((), ())), precision=precision, preferred_element_type=F32
    )


def dot_nt(left, right, precision=None):
    return dot(left, right, ((1,), (1,)), precision)


def dot_tn(left, right, precision=None):
    return dot(left, right, ((0,), (0,)), precision)


HIGH = lax.Precision.HIGHEST


def sin_cos(angle):
    turns = jnp.floor(angle * (2.0 / math.pi) + 0.5)
    rest = angle - turns * 1.5703125
    rest = rest - turns * 4.837512969970703125e-4
    rest = rest - turns * 7.54978995489188e-8
    square = rest * rest
    sine = rest + rest * square * (
        -1.6666654611e-1 + square * (8.3321608736e-3 + square * -1.9515295891e-4)
    )
    cosine = (
        1.0
        - 0.5 * square
        + square
        * square
        * (4.166664568298827e-2 + square * (-1.388731625493765e-3 + square * 2.443315711809948e-5))
    )
    half = jnp.floor(turns * 0.5)
    odd = turns - 2.0 * half
    sign = 1.0 - 2.0 * (half - 2.0 * jnp.floor(half * 0.5))
    swapped = odd > 0.5
    return (
        jnp.where(swapped, cosine, sine) * sign,
        jnp.where(swapped, -sine, cosine) * sign,
    )


def norm_parts(values):
    center = values - jnp.mean(values, axis=-1, keepdims=True)
    scale = lax.rsqrt(jnp.mean(center * center, axis=-1, keepdims=True) + EPS)
    return center * scale, scale


def norm_back(grad, gain, unit, scale):
    inner = grad * gain
    return scale * (
        inner
        - jnp.mean(inner, axis=-1, keepdims=True)
        - unit * jnp.mean(inner * unit, axis=-1, keepdims=True)
    )


def column(row):
    size = row.shape[1]
    same = lax.broadcasted_iota(jnp.int32, (size, size), 0) == lax.broadcasted_iota(
        jnp.int32, (size, size), 1
    )
    return jnp.sum(jnp.where(same, row, 0.0), axis=1, keepdims=True)


def fused(s, names, *refs):
    r = types.SimpleNamespace(**dict(zip(names, refs)))
    ranks, halves, inner, rows = s.ranks, s.halves, s.inner, s.rows
    channels, hidden = s.channels, s.hidden
    dp, mp = lax.axis_index("dp"), lax.axis_index("mp")
    y, c = dp // 2, dp % 2
    q, j = mp // halves, mp % halves
    other, across = 1 - c, 1 - q
    outer = halves // inner

    def device(yy, cc, qq, jj):
        return (yy * 2 + cc, qq * halves + jj)

    def ahead(k):
        return ((j // inner + k // inner) % outer) * inner + (j % inner + k % inner) % inner

    def behind(k):
        return ((j // inner + outer - k // inner) % outer) * inner + (
            j % inner + inner - k % inner
        ) % inner

    sibling = device(y, other, q, j)
    partner = device(y, other, across, j)
    moved = c != q

    def remote(src, dst, send, recv, target):
        return pltpu.make_async_remote_copy(
            src_ref=src,
            dst_ref=dst,
            send_sem=send,
            recv_sem=recv,
            device_id=target,
            device_id_type=MESH,
        )

    def block_rows(cc, jj):
        return pl.ds(pl.multiple_of((cc * halves + jj) * rows, rows), rows)

    mine = block_rows(c, j)

    barrier = pltpu.get_barrier_semaphore()
    greeted = [sibling, partner]
    for k in range(1, halves):
        greeted += [device(y, c, q, ahead(k)), device(y, other, q, ahead(k))]
    for dy in range(ranks):
        for dq in range(2):
            if dy or dq:
                greeted.append(device((y + dy) % ranks, c, (q + dq) % 2, j))
    for target in greeted:
        pl.semaphore_signal(barrier, inc=1, device_id=target, device_id_type=MESH)

    par = r.par_own
    par[...] = jnp.zeros_like(par)
    par[0:1, 0 : 3 * channels] = r.in_bias[...]
    par[1:4, 0 : 3 * channels] = r.short_taps[...]
    par[4:5, 0:channels] = r.skip_gain[...]
    par[5:6, 0:hidden] = r.up_bias[...].astype(F32)

    pl.semaphore_wait(barrier, len(greeted))

    takes = [
        (r.x_any, r.x_in),
        (par, r.par_in),
        (r.win_any, r.win),
        (r.og_any, r.og_in),
        (r.wout_any, r.wout.at[pl.ds(0, channels)]),
        (r.wup_any, r.wup),
        (r.wdn_any, r.wdn),
    ]

    def take(i):
        src, dst = takes[i]
        return remote(src, dst, r.take_send.at[i], r.take_recv.at[i], partner)

    def take_local(i):
        src, dst = takes[i]
        return pltpu.make_async_copy(src, dst, r.take_local.at[i])

    @pl.when(moved)
    def _():
        for i in range(len(takes)):
            take(i).start()

    @pl.when(jnp.logical_not(moved))
    def _():
        for i in range(len(takes)):
            take_local(i).start()

    def taken(*which):
        @pl.when(moved)
        def _():
            for i in which:
                take(i).wait_recv()

        @pl.when(jnp.logical_not(moved))
        def _():
            for i in which:
                take_local(i).wait()

    pack = y * 2 + q
    segments = []
    for i in range(COUNT):
        found = jnp.int32(-1)
        for k in range(s.sequences):
            start = r.offsets[k]
            hit = (
                (r.owners[k] == pack)
                & (start <= i * BLOCK)
                & (start + r.lengths[k] > i * BLOCK)
            )
            found = jnp.where(hit, jnp.int32(k), found)
        segments.append(found)
    valid = [jnp.where(seg >= 0, jnp.float32(1), jnp.float32(0)) for seg in segments]
    joined = [
        [valid[i] * jnp.where(segments[i] == segments[p], jnp.float32(1), jnp.float32(0)) for p in range(i + 1)]
        for i in range(COUNT)
    ]
    follows = [jnp.float32(0)] + [joined[i][i - 1] for i in range(1, COUNT)]

    row_index = lax.broadcasted_iota(jnp.int32, (3 * channels, WIDE), 0)
    lane_index = lax.broadcasted_iota(jnp.int32, (3 * channels, WIDE), 1)
    within = lane_index % LANES
    order = jnp.where(
        (row_index == 3 * within + lane_index // LANES) & (within < channels), 1.0, 0.0
    )
    r.order[...] = order.astype(BF16)
    r.order_wide[...] = order

    features = r.features[...]
    embed_freq, embed_bias = column(r.embed_freq[...]), column(r.embed_bias[...])
    hidden_freq, hidden_bias = column(r.hidden_freq[...]), column(r.hidden_bias[...])
    first_sum = dot_tn(r.embed_weight[...], features, HIGH) + embed_bias
    first, first_cos = sin_cos(embed_freq * first_sum)
    r.first_sum[...] = first_sum
    r.first[...] = first
    r.first_cos[...] = first_cos
    second_sum = dot_tn(r.hidden_weight[...], first, HIGH) + hidden_bias
    second, second_cos = sin_cos(hidden_freq * second_sum)
    r.second_sum[...] = second_sum
    r.second[...] = second
    r.second_cos[...] = second_cos
    shard = c * halves + j
    pick_row = lax.broadcasted_iota(jnp.int32, (D, LANES), 0)
    pick_lane = lax.broadcasted_iota(jnp.int32, (D, LANES), 1)
    pick = jnp.where((pick_row == shard * channels + pick_lane) & (pick_lane < channels), 1.0, 0.0)
    own_filter = dot(r.filter_weight[...], pick, precision=HIGH)
    own_decay = dot(jnp.broadcast_to(r.decay_rate[...], (8, D)), pick, precision=HIGH)[0:1]
    r.own_filter[...] = own_filter
    r.own_decay[...] = jnp.broadcast_to(own_decay, (8, LANES))
    r.spread[...] = jnp.zeros_like(r.spread)
    for i in range(COUNT):
        at = slice(i * BLOCK, (i + 1) * BLOCK)
        tau = (
            lax.broadcasted_iota(jnp.int32, (BLOCK, LANES), 0) + i * BLOCK
        ).astype(F32) * (1.0 / LONG)
        kernel = dot_tn(second[:, at], own_filter, HIGH) * jnp.exp(-tau * own_decay)
        r.kernel[at, :] = kernel
        low = kernel.astype(BF16)
        r.spread[0:BLOCK, i * LANES : (i + 1) * LANES] = low
        if i + 1 < COUNT:
            r.spread[BLOCK:BINS, (i + 1) * LANES : (i + 2) * LANES] = low
    r.kernel_wave[...] = dot(r.waves[...], r.spread[...])

    def gather_copies(n, held):
        out = []
        for k in range(1, halves):
            out.append(
                remote(
                    held.at[mine],
                    held.at[mine],
                    r.gather_send.at[n, k],
                    r.gather_recv.at[n, k],
                    device(y, c, q, ahead(k)),
                )
            )
        out.append(
            remote(
                held.at[mine],
                held.at[mine],
                r.gather_send.at[n, 0],
                r.gather_recv.at[n, 0],
                sibling,
            )
        )
        return out

    def gather_start(n, held):
        for copy in gather_copies(n, held):
            copy.start()

    def gather_finish(n, held):
        forwards = []
        for k in range(1, halves):
            came = held.at[block_rows(c, behind(k))]
            remote(
                came,
                came,
                r.gather_send.at[n, k],
                r.gather_recv.at[n, k],
                device(y, c, q, behind(k)),
            ).wait_recv()
            forward = remote(
                came, came, r.pass_send.at[n, k], r.pass_recv.at[n, k], sibling
            )
            forward.start()
            forwards.append(forward)
        for k in range(halves):
            came = held.at[block_rows(other, behind(k))]
            recv = r.pass_recv.at[n, k] if k else r.gather_recv.at[n, 0]
            remote(came, came, r.pass_send.at[n, k], recv, sibling).wait_recv()
        for copy in gather_copies(n, held) + forwards:
            copy.wait_send()

    def chip_copy(n, k):
        return remote(
            r.chip_out.at[n, k],
            r.chip_in.at[n, k],
            r.chip_send.at[n, k],
            r.chip_recv.at[n, k],
            sibling,
        )

    def link_copy(n, k):
        return remote(
            r.link_out.at[n, k],
            r.link_in.at[n, k],
            r.link_send.at[n, k],
            r.link_recv.at[n, k],
            device(y, c, q, ahead(k)),
        )

    def chip_give(n, k, value):
        r.chip_out[n, k] = value.astype(BF16)
        chip_copy(n, k).start()

    def chip_add(n, k, value):
        chip_copy(n, k).wait_recv()
        return value + r.chip_in[n, k].astype(F32)

    def scatter(n, part):
        def give(i, carry):
            k = (i + 1) % halves
            chip_give(n, k, part(block_rows(other, ahead(k))))
            return carry

        lax.fori_loop(0, halves, give, 0)

        def send(k, carry):
            r.link_out[n, k] = chip_add(n, k, part(block_rows(c, ahead(k)))).astype(BF16)
            link_copy(n, k).start()
            return carry

        lax.fori_loop(1, halves, send, 0)
        r.own_sum[n] = chip_add(n, 0, part(mine))

    def scatter_finish(n):
        total = r.own_sum[n]
        for k in range(1, halves):
            link_copy(n, k).wait_recv()
            total = total + r.link_in[n, k].astype(F32)
        for k in range(halves):
            chip_copy(n, k).wait_send()
            if k:
                link_copy(n, k).wait_send()
        return total

    taken(0)
    unit, _ = norm_parts(r.x_in[...].astype(F32))
    r.g_one[mine, :] = (unit * r.mixer_gain[...]).astype(BF16)
    gather_start(0, r.g_one)
    taken(1, 2)
    par_wide = dot(par_in_rows(r.par_in, channels), r.order_wide[...], precision=HIGH)
    r.taps[...] = par_wide
    for i in range(3):
        at = slice(i * BLOCK, (i + 1) * BLOCK)
        r.win_apart[at, :] = dot(r.win[at, :], r.order[...]).astype(BF16)
    r.wout[channels:, :] = jnp.zeros_like(r.wout[channels:, :])
    gather_finish(0, r.g_one)

    taken(3)
    r.g_out[mine, :] = r.og_in[...]
    gather_start(1, r.g_out)

    def project(i, carry):
        at = pl.ds(pl.multiple_of(i * LANES, LANES), LANES)
        r.projected[at, :] = dot(r.g_one[at, :], r.win_apart[...]) + r.taps[0:1, :]
        return carry

    lax.fori_loop(0, LONG // LANES, project, 0)

    rows_here = lax.broadcasted_iota(jnp.int32, (BLOCK, 1), 0)

    def back_rows(i):
        now = r.projected[i * BLOCK : (i + 1) * BLOCK, :]
        one, two = pltpu.roll(now, 1, 0), pltpu.roll(now, 2, 0)
        if i:
            edge = r.projected[i * BLOCK - 8 : i * BLOCK, :] * follows[i]
            last, before = edge[7:8], edge[6:7]
        else:
            last = before = jnp.zeros((1, WIDE), F32)
        one = jnp.where(rows_here == 0, last, one)
        two = jnp.where(rows_here == 0, before, jnp.where(rows_here == 1, last, two))
        return now, one, two

    for i in range(COUNT):
        now, one, two = back_rows(i)
        short = r.taps[1:2, :] * now + r.taps[2:3, :] * one + r.taps[3:4, :] * two
        r.short[i * BLOCK : (i + 1) * BLOCK, :] = short
        signal = short[:, 2 * LANES :] * short[:, LANES : 2 * LANES] * valid[i]
        r.signal[:, i * LANES : (i + 1) * LANES] = signal.astype(BF16)

    near = r.waves[:, 0:BLOCK]
    unnear = r.unwaves[:, 0:BINS]
    r.signal_wave[...] = dot(near, r.signal[...])
    step = 16

    def load_wave(ref, at, count=COUNT):
        low, high = pl.ds(at, step), pl.ds(at + BLOCK, step)
        return [
            (ref[low, i * LANES : (i + 1) * LANES], ref[high, i * LANES : (i + 1) * LANES])
            for i in range(count)
        ]

    def store_wave(ref, base, at, i, pair):
        ref[pl.ds(base + at, step), i * LANES : (i + 1) * LANES] = pair[0].astype(BF16)
        ref[pl.ds(base + at + BLOCK, step), i * LANES : (i + 1) * LANES] = pair[1].astype(BF16)

    def weighted(terms):
        real = imag = None
        for weight, (a, b) in terms:
            real = a * weight if real is None else real + a * weight
            imag = b * weight if imag is None else imag + b * weight
        return real, imag

    def times(left, right):
        return left[0] * right[0] - left[1] * right[1], left[0] * right[1] + left[1] * right[0]

    def times_conj(left, right):
        return left[0] * right[0] + left[1] * right[1], left[0] * right[1] - left[1] * right[0]

    def forward_wave(n, carry):
        at = pl.multiple_of(n * step, step)
        kernels, signals = load_wave(r.kernel_wave, at), load_wave(r.signal_wave, at)
        for i in range(COUNT):
            store_wave(
                r.product,
                0,
                at,
                i,
                weighted([(joined[i][p], times(kernels[i - p], signals[p])) for p in range(i + 1)]),
            )
        return carry

    lax.fori_loop(0, BLOCK // step, forward_wave, 0)
    skip = r.par_in[4:5, 0:LANES]
    convolved = dot(unnear, r.product[0:BINS, :])
    for i in range(COUNT):
        at = slice(i * BLOCK, (i + 1) * BLOCK)
        lanes = slice(i * LANES, (i + 1) * LANES)
        direct = convolved[:, lanes] + skip * r.signal[:, lanes].astype(F32)
        r.direct[at, :] = direct
        r.mixed[at, :] = (direct * r.short[at, 0:LANES]).astype(BF16)

    taken(4)
    scatter(0, lambda at: dot(r.mixed[at, :], r.wout[...]))
    gather_finish(1, r.g_out)
    middle = r.x_in[...].astype(F32) + r.out_bias[...] + scatter_finish(0)
    r.middle[...] = middle
    unit, _ = norm_parts(middle)
    r.g_two[mine, :] = (unit * r.ffn_gain[...]).astype(BF16)
    gather_start(2, r.g_two)
    taken(5, 6)
    gather_finish(2, r.g_two)

    def feed(at):
        value = dot(r.g_two[at, :], r.wup[...]) + r.par_in[5:6, 0:hidden]
        square = value * value
        bend = jnp.tanh(ROOT * value * (1.0 + CUBE * square))
        half = 0.5 * (1.0 + bend)
        active = (value * half).astype(BF16)
        slope = half + 0.5 * value * (1.0 - bend * bend) * (ROOT * (1.0 + 3.0 * CUBE * square))
        grad = (slope * dot_nt(r.g_out[at, :], r.wdn[...])).astype(BF16)
        r.active[at, :] = active
        r.hidden_grad[at, :] = grad
        return dot_nt(grad, r.wup[...]), dot(active, r.wdn[...])

    def feed_give(i, carry):
        k = (i + 1) % halves
        back, forth = feed(block_rows(other, ahead(k)))
        chip_give(1, k, back)
        chip_give(2, k, forth)
        return carry

    lax.fori_loop(0, halves, feed_give, 0)

    def feed_send(k, carry):
        back, forth = feed(block_rows(c, ahead(k)))
        r.link_out[1, k] = chip_add(1, k, back).astype(BF16)
        link_copy(1, k).start()
        r.link_out[2, k] = chip_add(2, k, forth).astype(BF16)
        return carry

    lax.fori_loop(1, halves, feed_send, 0)
    back, forth = feed(mine)
    r.own_sum[1] = chip_add(1, 0, back)
    r.own_sum[2] = chip_add(2, 0, forth)

    sums = [
        (r.grad_in, r.part_in, r.y_in, r.z_in, r.gwin),
        (r.grad_out, r.part_out, r.y_out, r.z_out, r.gwout),
        (r.grad_up, r.part_up, r.y_up, r.z_up, r.gwup),
        (r.grad_dn, r.part_dn, r.y_dn, r.z_dn, r.gwdn),
    ]
    owner = jnp.logical_not(moved)

    def part_rows(ref, yy):
        size = ref.shape[0] // ranks
        return pl.ds(pl.multiple_of(yy * size, 16), size)

    def y_copy(w, dy):
        full, _, came, _, _ = sums[w]
        to = (y + dy) % ranks
        return remote(
            full.at[part_rows(full, to)],
            came.at[dy],
            r.y_send.at[w, dy],
            r.y_recv.at[w, dy],
            device(to, c, q, j),
        )

    def z_copy(w):
        _, part, _, came, _ = sums[w]
        return remote(
            part, came, r.z_send.at[w], r.z_recv.at[w], device(y, c, across, j)
        )

    def out_copy(w, dy):
        final = sums[w][4]
        at = part_rows(final, y)
        return remote(
            final.at[at],
            final.at[at],
            r.out_send.at[w, dy],
            r.out_recv.at[w, dy],
            device((y + dy) % ranks, c, q, j),
        )

    def chip_final(w, dy):
        final = sums[w][4]
        at = part_rows(final, (y + ranks - dy) % ranks)
        return remote(
            final.at[at],
            final.at[at],
            r.fin_send.at[w, dy],
            r.fin_recv.at[w, dy],
            sibling,
        )

    def sum_start(w):
        for dy in range(1, ranks):
            y_copy(w, dy).start()

    def sum_cross(w):
        full, part, came, _, _ = sums[w]
        total = full[part_rows(full, y), :].astype(F32)
        for dy in range(1, ranks):
            y_copy(w, dy).wait_recv()
            total = total + came[dy].astype(F32)
        part[...] = total.astype(BF16)

        @pl.when(moved)
        def _():
            z_copy(w).start()

    def sum_close(w):
        _, part, _, came, final = sums[w]

        @pl.when(owner)
        def _():
            z_copy(w).wait_recv()
            final[part_rows(final, y), :] = (
                part[...].astype(F32) + came[...].astype(F32)
            ).astype(BF16)
            for dy in range(1, ranks):
                out_copy(w, dy).start()
            chip_final(w, 0).start()

    def sum_finish(w):
        final = sums[w][4]

        @pl.when(owner)
        def _():
            for dy in range(1, ranks):
                at = part_rows(final, (y + ranks - dy) % ranks)
                remote(
                    final.at[at],
                    final.at[at],
                    r.out_send.at[w, dy],
                    r.out_recv.at[w, dy],
                    sibling,
                ).wait_recv()
                chip_final(w, dy).start()
            for dy in range(1, ranks):
                out_copy(w, dy).wait_send()
            for dy in range(ranks):
                chip_final(w, dy).wait_send()

        @pl.when(moved)
        def _():
            for dy in range(ranks):
                chip_final(w, dy).wait_recv()
            z_copy(w).wait_send()

        for dy in range(1, ranks):
            y_copy(w, dy).wait_send()

    def weight_grad(target, left, right, by_right=False):
        def chunk(i, carry):
            at = pl.ds(pl.multiple_of(i * BLOCK, BLOCK), BLOCK)
            if by_right:
                target[0 : left.shape[1], at] = dot_tn(left[...], right[:, at]).astype(BF16)
            else:
                target[at, :] = dot_tn(left[:, at], right[...]).astype(BF16)
            return carry

        lax.fori_loop(0, D // BLOCK, chunk, 0)

    if r.grad_dn.shape[0] > hidden:
        r.grad_dn[hidden:, :] = jnp.zeros_like(r.grad_dn[hidden:, :])
    weight_grad(r.grad_dn, r.active, r.g_out, True)
    sum_start(3)
    weight_grad(r.grad_up, r.g_two, r.hidden_grad)
    sum_start(2)

    ffn_back = scatter_finish(1)
    seed = r.og_in[...].astype(F32)
    unit, scale = norm_parts(r.middle[...])
    middle_grad = seed + norm_back(ffn_back, r.ffn_gain[...], unit, scale)
    r.middle_grad[...] = middle_grad
    branch_grad = middle_grad.astype(BF16)
    r.g_back[mine, :] = branch_grad
    gather_start(3, r.g_back)
    vectors = [
        jnp.sum(ffn_back * unit, axis=0, keepdims=True),
        jnp.sum(branch_grad.astype(F32), axis=0, keepdims=True),
        jnp.sum(seed, axis=0, keepdims=True),
    ]
    r.pay[...] = jnp.zeros_like(r.pay)
    for v, vector in enumerate(vectors):
        for k in range(D // LANES):
            at = PAY_VEC + v * (D // LANES) + k
            r.pay[at : at + 1, :] = vector[:, k * LANES : (k + 1) * LANES]
    par_grad = r.par_grad
    par_grad[...] = jnp.zeros_like(par_grad)
    par_grad[5:6, 0:hidden] = jnp.sum(r.hidden_grad[...].astype(F32), axis=0, keepdims=True)
    sum_cross(3)
    sum_cross(2)
    gather_finish(3, r.g_back)
    for k in range(1, halves):
        link_copy(2, k).start()

    skip_total = jnp.zeros((1, LANES), F32)
    for i in range(COUNT):
        at = slice(i * BLOCK, (i + 1) * BLOCK)
        lanes = slice(i * LANES, (i + 1) * LANES)
        mixed_grad = dot_nt(r.g_back[at, :], r.wout[...])
        r.short_grad[at, 0:LANES] = mixed_grad * r.direct[at, :]
        direct_grad = mixed_grad * r.short[at, 0:LANES]
        r.direct[at, :] = direct_grad
        r.direct_low[:, lanes] = direct_grad.astype(BF16)
        skip_total += jnp.sum(
            direct_grad * r.signal[:, lanes].astype(F32), axis=0, keepdims=True
        )
    par_grad[4:5, 0:LANES] = skip_total
    r.grad_wave[...] = dot(near, r.direct_low[...])
    r.back_product[...] = jnp.zeros_like(r.back_product)

    def backward_wave(n, carry):
        at = pl.multiple_of(n * step, step)
        kernels, signals = load_wave(r.kernel_wave, at), load_wave(r.signal_wave, at)
        grads = load_wave(r.grad_wave, at)
        for p in range(COUNT):
            terms = [(joined[i][p], times_conj(kernels[i - p], grads[i])) for i in range(p, COUNT)]
            store_wave(r.product, 0, at, p, weighted(terms))
        for d in range(COUNT):
            terms = [
                (joined[i][i - d], times_conj(signals[i - d], grads[i])) for i in range(d, COUNT)
            ]
            pair = weighted(terms)
            store_wave(r.back_product, 0, at, d, pair)
            if d:
                store_wave(r.back_product, BINS, at, d - 1, pair)
        return carry

    lax.fori_loop(0, BLOCK // step, backward_wave, 0)
    signal_grads = dot(unnear, r.product[0:BINS, :])
    for i in range(COUNT):
        at = slice(i * BLOCK, (i + 1) * BLOCK)
        lanes = slice(i * LANES, (i + 1) * LANES)
        signal_grad = (signal_grads[:, lanes] + skip * r.direct[at, :]) * valid[i]
        r.short_grad[at, LANES : 2 * LANES] = signal_grad * r.short[at, 2 * LANES :]
        r.short_grad[at, 2 * LANES :] = signal_grad * r.short[at, LANES : 2 * LANES]

    bias_total = jnp.zeros((1, WIDE), F32)
    tap_totals = [jnp.zeros((1, WIDE), F32) for _ in range(3)]
    for i in range(COUNT):
        at = slice(i * BLOCK, (i + 1) * BLOCK)
        now, one, two = back_rows(i)
        grad = r.short_grad[at, :]
        for t, value in enumerate((now, one, two)):
            tap_totals[t] += jnp.sum(grad * value, axis=0, keepdims=True)
        next_one = pltpu.roll(grad, BLOCK - 1, 0)
        next_two = pltpu.roll(grad, BLOCK - 2, 0)
        if i + 1 < COUNT:
            edge = r.short_grad[(i + 1) * BLOCK : (i + 1) * BLOCK + 8, :] * follows[i + 1]
            head, after = edge[0:1], edge[1:2]
        else:
            head = after = jnp.zeros((1, WIDE), F32)
        next_one = jnp.where(rows_here == BLOCK - 1, head, next_one)
        next_two = jnp.where(
            rows_here == BLOCK - 2, head, jnp.where(rows_here == BLOCK - 1, after, next_two)
        )
        low = (
            r.taps[1:2, :] * grad + r.taps[2:3, :] * next_one + r.taps[3:4, :] * next_two
        ).astype(BF16)
        bias_total += jnp.sum(low.astype(F32), axis=0, keepdims=True)
        r.projected_grad[at, :] = dot_nt(low, r.order[...]).astype(BF16)
    par_grad[0:1, :] = bias_total
    for t in range(3):
        par_grad[t + 1 : t + 2, :] = tap_totals[t]

    scatter(3, lambda at: dot_nt(r.projected_grad[at, :], r.win[...]))

    weight_grad(r.grad_in, r.g_one, r.projected_grad)
    sum_start(0)
    r.grad_out[...] = dot_tn(r.mixed[...], r.g_back[...]).astype(BF16)
    sum_start(1)
    sum_close(3)
    sum_close(2)

    kernel_grads = dot(r.unwaves[...], r.back_product[...])
    decay_total = jnp.zeros((1, LANES), F32)
    penalty = jnp.zeros((1, LANES), F32)
    own_filter = r.own_filter[...]
    own_decay = r.own_decay[0:1, :]
    lead = jnp.where(pack == 0, 1.0 / D, 0.0).astype(F32)
    for i in range(COUNT):
        at = slice(i * BLOCK, (i + 1) * BLOCK)
        tau = (
            lax.broadcasted_iota(jnp.int32, (BLOCK, LANES), 0) + i * BLOCK
        ).astype(F32) * (1.0 / LONG)
        kernel = r.kernel[at, :]
        weighed = tau * kernel
        penalty += jnp.sum(weighed * kernel, axis=0, keepdims=True) * lead
        kernel_grad = (
            kernel_grads[:, i * LANES : (i + 1) * LANES] + weighed * (2.0 * lead)
        )
        decay_total -= jnp.sum(kernel_grad * weighed, axis=0, keepdims=True)
        r.raw_grad[at, :] = kernel_grad * jnp.exp(-tau * own_decay)
    shard_sum = r.shard_sum
    slot = y * 2 + q
    shard_sum[slot] = jnp.zeros((SHARD_ROWS, LANES), F32)
    shard_sum[slot, 0:FILT, :] = dot(r.second[...], r.raw_grad[...], precision=HIGH)
    shard_sum[slot, SHARD_DECAY : SHARD_DECAY + 1, :] = decay_total
    for k in range(3):
        at = SHARD_PAR + 8 * k
        shard_sum[slot, at : at + 8, :] = par_grad[:, k * LANES : (k + 1) * LANES]
    r.pay[PAY_PEN : PAY_PEN + 1, :] = penalty
    second_grad = dot_nt(own_filter, r.raw_grad[...], HIGH)
    angle_grad = second_grad * r.second_cos[...]
    freq_grad = jnp.sum(angle_grad * r.second_sum[...], axis=1, keepdims=True)
    sum_grad = angle_grad * column(r.hidden_freq[...])
    at = slice(PAY_HID, PAY_HID + FILT)
    r.pay[at, 0:FILT] = dot_nt(r.first[...], sum_grad, HIGH)
    r.pay[at, FILT : FILT + 1] = freq_grad
    r.pay[at, FILT + 1 : FILT + 2] = jnp.sum(sum_grad, axis=1, keepdims=True)
    angle_grad = dot(r.hidden_weight[...], sum_grad, precision=HIGH) * r.first_cos[...]
    r.pay[at, FILT + 2 : FILT + 3] = jnp.sum(
        angle_grad * r.first_sum[...], axis=1, keepdims=True
    )
    sum_grad = angle_grad * column(r.embed_freq[...])
    r.pay[at, FILT + 3 : FILT + 4] = jnp.sum(sum_grad, axis=1, keepdims=True)
    r.pay[PAY_EMB : PAY_EMB + EMB, 0:FILT] = dot_nt(features, sum_grad, HIGH)

    def pay_chip(n, src, dst):
        return remote(src, dst, r.pay_send.at[n, 0], r.pay_recv.at[n, 0], sibling)

    def pay_links(n, held):
        return [
            remote(
                held.at[j],
                held.at[j],
                r.pay_send.at[n, k],
                r.pay_recv.at[n, k],
                device(y, c, q, ahead(k)),
            )
            for k in range(1, halves)
        ]

    def pay_packs(n, held):
        out = []
        for dy in range(ranks):
            for dq in range(2):
                if dy or dq:
                    out.append(
                        remote(
                            held.at[slot],
                            held.at[slot],
                            r.cross_send.at[n, dy * 2 + dq],
                            r.cross_recv.at[n, dy * 2 + dq],
                            device((y + dy) % ranks, c, (q + dq) % 2, j),
                        )
                    )
        return out

    def pay_packs_wait(n, held):
        total = None
        for dy in range(ranks):
            for dq in range(2):
                if dy or dq:
                    yy, qq = (y + ranks - dy) % ranks, (q + dq) % 2
                    came = held.at[yy * 2 + qq]
                    remote(
                        came,
                        came,
                        r.cross_send.at[n, dy * 2 + dq],
                        r.cross_recv.at[n, dy * 2 + dq],
                        device(yy, c, qq, j),
                    ).wait_recv()
        for i in range(2 * ranks):
            total = held[i] if total is None else total + held[i]
        return total

    def pay_group(n, own, chip_in, held):
        first_copy = pay_chip(n, own, chip_in)
        first_copy.wait_recv()
        held[j] = own[...] + chip_in[...]
        for copy in pay_links(n, held):
            copy.start()

    def pay_group_wait(n, held):
        for k in range(1, halves):
            came = held.at[behind(k)]
            remote(
                came,
                came,
                r.pay_send.at[n, k],
                r.pay_recv.at[n, k],
                device(y, c, q, behind(k)),
            ).wait_recv()
        total = held[0]
        for i in range(1, halves):
            total = total + held[i]
        return total

    for copy in pay_packs(2, shard_sum):
        copy.start()
    pay_chip(0, r.pay, r.pay_in).start()
    sum_cross(0)
    sum_cross(1)
    pay_group(0, r.pay, r.pay_in, r.pay_held)

    mixer_back = scatter_finish(3)
    unit, scale = norm_parts(r.x_in[...].astype(F32))
    r.input_grad[...] = r.middle_grad[...] + norm_back(
        mixer_back, r.mixer_gain[...], unit, scale
    )
    r.block_out[...] = (
        r.middle[...] + r.down_bias[...] + scatter_finish(2)
    ).astype(BF16)
    gives = [(r.input_grad, r.input_any), (r.block_out, r.block_any)]

    def give(i):
        src, dst = gives[i]
        return remote(src, dst, r.give_send.at[i], r.give_recv.at[i], partner)

    def give_local(i):
        src, dst = gives[i]
        return pltpu.make_async_copy(src, dst, r.give_local.at[i])

    @pl.when(moved)
    def _():
        for i in range(len(gives)):
            give(i).start()

    @pl.when(owner)
    def _():
        for i in range(len(gives)):
            give_local(i).start()

    gain_row = jnp.sum(mixer_back * unit, axis=0, keepdims=True)
    r.late[...] = jnp.zeros_like(r.late)
    for k in range(D // LANES):
        r.late[k : k + 1, :] = gain_row[:, k * LANES : (k + 1) * LANES]
    pay_chip(1, r.late, r.late_in).start()
    sum_close(0)
    sum_close(1)
    r.pay_cross[slot] = pay_group_wait(0, r.pay_held)
    for copy in pay_packs(0, r.pay_cross):
        copy.start()
    pay_group(1, r.late, r.late_in, r.late_held)

    r.shards[shard] = pay_packs_wait(2, shard_sum)

    def shard_copies():
        held = r.shards
        out = [
            remote(
                held.at[shard],
                held.at[shard],
                r.gather_send.at[4, k],
                r.gather_recv.at[4, k],
                device(y, c, q, ahead(k)) if k else sibling,
            )
            for k in range(halves)
        ]
        return out

    for copy in shard_copies():
        copy.start()
    r.late_cross[slot] = pay_group_wait(1, r.late_held)
    for copy in pay_packs(1, r.late_cross):
        copy.start()
    forwards = []
    for k in range(1, halves):
        came = r.shards.at[c * halves + behind(k)]
        remote(
            came,
            came,
            r.gather_send.at[4, k],
            r.gather_recv.at[4, k],
            device(y, c, q, behind(k)),
        ).wait_recv()
        forward = remote(came, came, r.pass_send.at[4, k], r.pass_recv.at[4, k], sibling)
        forward.start()
        forwards.append(forward)
    for k in range(halves):
        came = r.shards.at[other * halves + behind(k)]
        recv = r.pass_recv.at[4, k] if k else r.gather_recv.at[4, 0]
        remote(came, came, r.pass_send.at[4, k], recv, sibling).wait_recv()
    r.pay_total[...] = pay_packs_wait(0, r.pay_cross)
    home = r.shards[q * halves + j]
    wide = jnp.concatenate(
        [home[SHARD_PAR + 8 * k : SHARD_PAR + 8 * k + 8] for k in range(3)], axis=1
    )
    r.par_wide[...] = wide
    r.par_close[...] = dot_nt(wide, r.order_wide[...], HIGH)
    r.late_total[...] = pay_packs_wait(1, r.late_cross)
    for w in (3, 2, 1, 0):
        sum_finish(w)

    for copy in shard_copies() + forwards:
        copy.wait_send()
    for n, own, chip_in, held, cross in (
        (0, r.pay, r.pay_in, r.pay_held, r.pay_cross),
        (1, r.late, r.late_in, r.late_held, r.late_cross),
    ):
        pay_chip(n, own, chip_in).wait_send()
        for copy in pay_links(n, held) + pay_packs(n, cross):
            copy.wait_send()
    for copy in pay_packs(2, shard_sum):
        copy.wait_send()

    @pl.when(moved)
    def _():
        for i in range(len(takes)):
            take(i).wait_send()
        for i in range(len(gives)):
            give(i).wait()

    @pl.when(owner)
    def _():
        for i in range(len(gives)):
            give_local(i).wait()


def par_in_rows(ref, channels):
    return ref[:, 0 : 3 * channels]


def round_up(value, unit):
    return (value + unit - 1) // unit * unit


def solution(mesh):
    n_dp, n_mp = mesh.shape["dp"], mesh.shape["mp"]

    def per_device(
        block_input,
        mixer_gain,
        in_weight,
        in_bias,
        short_taps,
        skip_gain,
        out_weight,
        out_bias,
        ffn_gain,
        up_weight,
        up_bias,
        down_weight,
        down_bias,
        embed_weight,
        embed_bias,
        embed_freq,
        hidden_weight,
        hidden_bias,
        hidden_freq,
        filter_weight,
        decay_rate,
        out_grad,
        sequence_lengths,
        sequence_rank,
        sequence_offset,
    ):
        ranks, halves = n_dp // 2, n_mp // 2
        rows = block_input.shape[0]
        channels, hidden = skip_gain.shape[0], up_weight.shape[1]
        sizes = types.SimpleNamespace(
            ranks=ranks,
            halves=halves,
            inner=n_mp // 4,
            rows=rows,
            channels=channels,
            hidden=hidden,
            sequences=sequence_lengths.shape[0],
        )
        down_rows = round_up(hidden, 16 * ranks)
        group = 2 * halves
        anywhere = pl.BlockSpec(memory_space=pl.ANY)
        vector = pl.BlockSpec(memory_space=pltpu.VMEM)
        scalar = pl.BlockSpec(memory_space=pltpu.SMEM)
        row = lambda value: value.reshape(1, -1)
        inputs = [
            ("x_any", block_input, anywhere),
            ("og_any", out_grad, anywhere),
            ("win_any", in_weight, anywhere),
            ("wout_any", out_weight, anywhere),
            ("wup_any", up_weight, anywhere),
            ("wdn_any", down_weight, anywhere),
            ("mixer_gain", row(mixer_gain), vector),
            ("ffn_gain", row(ffn_gain), vector),
            ("out_bias", row(out_bias), vector),
            ("down_bias", row(down_bias), vector),
            ("in_bias", row(in_bias), vector),
            ("short_taps", short_taps, vector),
            ("skip_gain", row(skip_gain), vector),
            ("up_bias", row(up_bias), vector),
            ("embed_weight", embed_weight, vector),
            ("embed_bias", row(embed_bias), vector),
            ("embed_freq", row(embed_freq), vector),
            ("hidden_weight", hidden_weight, vector),
            ("hidden_bias", row(hidden_bias), vector),
            ("hidden_freq", row(hidden_freq), vector),
            ("filter_weight", filter_weight, vector),
            ("decay_rate", row(decay_rate), vector),
            ("waves", jnp.asarray(WAVES, BF16), vector),
            ("unwaves", jnp.asarray(UNWAVES, BF16), vector),
            ("features", jnp.asarray(position_features(), F32), vector),
            ("lengths", sequence_lengths, scalar),
            ("owners", sequence_rank, scalar),
            ("offsets", sequence_offset, scalar),
        ]
        outputs = [
            ("block_any", (rows, D), BF16, anywhere),
            ("input_any", (rows, D), F32, anywhere),
            ("gwin", (D, 3 * channels), BF16, vector),
            ("gwout", (LANES, D), BF16, vector),
            ("gwup", (D, hidden), BF16, vector),
            ("gwdn", (down_rows, D), BF16, vector),
            ("pay_total", (PAY_ROWS, LANES), F32, vector),
            ("late_total", (8, LANES), F32, vector),
            ("shards", (group, SHARD_ROWS, LANES), F32, vector),
            ("par_wide", (8, WIDE), F32, vector),
            ("par_close", (8, 3 * channels), F32, vector),
        ]
        dma = pltpu.SemaphoreType.DMA
        scratch = {}

        def hold(name, shape, dtype=F32):
            scratch[name] = pltpu.VMEM(shape, dtype)

        hold("x_in", (rows, D), BF16)
        hold("og_in", (rows, D), BF16)
        hold("par_own", (8, WIDE))
        hold("par_in", (8, WIDE))
        hold("par_grad", (8, WIDE))
        hold("taps", (8, WIDE))
        hold("win", (D, 3 * channels), BF16)
        hold("win_apart", (D, WIDE), BF16)
        hold("wout", (LANES, D), BF16)
        hold("wup", (D, hidden), BF16)
        hold("wdn", (hidden, D), BF16)
        hold("order", (3 * channels, WIDE), BF16)
        hold("order_wide", (3 * channels, WIDE))
        for name in ("first", "first_sum", "first_cos", "second", "second_sum", "second_cos"):
            hold(name, (FILT, LONG))
        hold("own_filter", (FILT, LANES))
        hold("own_decay", (8, LANES))
        hold("kernel", (LONG, LANES))
        hold("raw_grad", (LONG, LANES))
        hold("spread", (BINS, COUNT * LANES), BF16)
        for name in ("kernel_wave", "signal_wave", "grad_wave"):
            hold(name, (BINS, COUNT * LANES))
        hold("product", (BINS, COUNT * LANES), BF16)
        hold("back_product", (2 * BINS, COUNT * LANES), BF16)
        for name in ("g_one", "g_out", "g_two", "g_back"):
            hold(name, (LONG, D), BF16)
        for name in ("projected", "short", "short_grad"):
            hold(name, (LONG, WIDE))
        hold("signal", (BLOCK, COUNT * LANES), BF16)
        hold("direct_low", (BLOCK, COUNT * LANES), BF16)
        hold("direct", (LONG, LANES))
        hold("mixed", (LONG, LANES), BF16)
        hold("middle", (rows, D))
        hold("middle_grad", (rows, D))
        hold("input_grad", (rows, D))
        hold("block_out", (rows, D), BF16)
        hold("active", (LONG, hidden), BF16)
        hold("hidden_grad", (LONG, hidden), BF16)
        hold("projected_grad", (LONG, 3 * channels), BF16)
        for name in ("chip_out", "chip_in", "link_out", "link_in"):
            hold(name, (4, halves, rows, D), BF16)
        hold("own_sum", (4, rows, D))
        for name, full in (
            ("in", (D, 3 * channels)),
            ("out", (LANES, D)),
            ("up", (D, hidden)),
            ("dn", (down_rows, D)),
        ):
            part = (full[0] // ranks, full[1])
            hold("grad_" + name, full, BF16)
            hold("part_" + name, part, BF16)
            hold("y_" + name, (ranks,) + part, BF16)
            hold("z_" + name, part, BF16)
        hold("pay", (PAY_ROWS, LANES))
        hold("pay_in", (PAY_ROWS, LANES))
        hold("pay_held", (halves, PAY_ROWS, LANES))
        hold("pay_cross", (2 * ranks, PAY_ROWS, LANES))
        hold("late", (8, LANES))
        hold("late_in", (8, LANES))
        hold("late_held", (halves, 8, LANES))
        hold("late_cross", (2 * ranks, 8, LANES))
        hold("shard_sum", (2 * ranks, SHARD_ROWS, LANES))
        for name, shape in (
            ("take", (7,)),
            ("give", (2,)),
            ("gather", (5, halves)),
            ("pass", (5, halves)),
            ("chip", (4, halves)),
            ("link", (4, halves)),
            ("y", (4, ranks)),
            ("z", (4,)),
            ("out", (4, ranks)),
            ("fin", (4, ranks)),
            ("pay", (2, halves)),
            ("cross", (3, 2 * ranks)),
        ):
            scratch[name + "_send"] = dma(shape)
            scratch[name + "_recv"] = dma(shape)
        scratch["take_local"] = dma((7,))
        scratch["give_local"] = dma((2,))
        names = [i[0] for i in inputs] + [o[0] for o in outputs] + list(scratch)
        results = pl.pallas_call(
            functools.partial(fused, sizes, names),
            out_shape=[jax.ShapeDtypeStruct(o[1], o[2]) for o in outputs],
            in_specs=[i[2] for i in inputs],
            out_specs=[o[3] for o in outputs],
            scratch_shapes=list(scratch.values()),
            compiler_params=pltpu.CompilerParams(
                collective_id=0,
                has_side_effects=True,
                vmem_limit_bytes=60 * 2**20,
            ),
            name="block",
        )(*[i[1] for i in inputs])
        out = dict(zip([o[0] for o in outputs], results))
        pay, shards = out["pay_total"], out["shards"]
        lines = D // LANES

        def shared(at):
            return pay[at : at + lines].reshape(D)

        def vector_of(k):
            return pay[PAY_HID : PAY_HID + FILT, FILT + k]

        return (
            out["block_any"],
            out["input_any"],
            jnp.sum(pay[PAY_PEN]),
            out["late_total"][0:lines].reshape(D),
            out["gwin"].astype(F32),
            out["par_close"][0],
            out["par_close"][1:4],
            out["par_wide"][4, 0:channels],
            out["gwout"][0:channels].astype(F32),
            shared(PAY_VEC + lines),
            shared(PAY_VEC),
            out["gwup"].astype(F32),
            out["par_wide"][5, 0:hidden],
            out["gwdn"][0:hidden].astype(F32),
            shared(PAY_VEC + 2 * lines),
            pay[PAY_EMB : PAY_EMB + EMB, 0:FILT],
            vector_of(3),
            vector_of(2),
            pay[PAY_HID : PAY_HID + FILT, 0:FILT],
            vector_of(1),
            vector_of(0),
            shards[:, 0:FILT, 0:channels].transpose(1, 0, 2).reshape(FILT, D),
            shards[:, SHARD_DECAY, 0:channels].reshape(D),
        )

    placed = (
        P(("dp", "mp"), None),
        P(),
        P(None, "mp"),
        P("mp"),
        P(None, "mp"),
        P("mp"),
        P("mp", None),
        P(),
        P(),
        P(None, "mp"),
        P("mp"),
        P("mp", None),
        P(),
        P(),
        P(),
        P(),
        P(),
        P(),
        P(),
        P(),
        P(),
        P(("dp", "mp"), None),
        P(),
        P(),
        P(),
    )
    return jax.shard_map(
        per_device,
        mesh=mesh,
        in_specs=placed,
        out_specs=(
            P(("dp", "mp"), None),
            P(("dp", "mp"), None),
            P(),
            P(),
            P(None, "mp"),
            P("mp"),
            P(None, "mp"),
            P("mp"),
            P("mp", None),
            P(),
            P(),
            P(None, "mp"),
            P("mp"),
            P("mp", None),
            P(),
            P(),
            P(),
            P(),
            P(),
            P(),
            P(),
            P(),
            P(),
        ),
        check_vma=False,
    )
```

time: 2190 us -> 212 us (0.10)
  other arithmetic: 797 us -> 4.2 us
  local copies, waits for them, and re-layouts: 663 us -> 26.5 us
  waiting for transfers between devices: 512 us -> 0 us
  Pallas kernels: 0 us -> 179 us
  matrix products: 118 us -> 0 us
  blocking collectives: 48.9 us -> 0 us
    scatter-add x8 -> x0, other arithmetic: 706 us -> none  [visit(): toeplitz = jnp.take(window, lag_table, axis=1)]
    gather x16 -> x0, local copies, waits for them, and re-layouts: 513 us -> none  [visit(): toeplitz = jnp.take(window, lag_table, axis=1)]
    reduce_scatter x4 -> x0, waiting for transfers between devices: 252 us -> none  [the longest x1 65.9 us: per_device(): lax.psum_scatter(matmul(active_low, down_weight).astype(jnp.bfloat16), 'm...]
    pallas_call x0 -> x1, Pallas kernels: none -> 179 us  [per_device(): pl.pallas_call(functools.partial(fused, sizes, names), out_shape=[jax.Sha...]
    all_gather x4 -> x0, waiting for transfers between devices: 144 us -> none  [the longest x1 42.3 us: per_device(): gathered_two = lax.all_gather(normed_two_low, 'mp', axis=0, tiled=True)]
    dot_general x44 -> x0, matrix products: 118 us -> none  [the longest x24 80 us: visit(): jnp.einsum('cts,cis->cit', toeplitz, shifted, preferred_element_type=jnp....]
    psum x2 -> x0, waiting for transfers between devices: 105 us -> none  [the longest x1 83 us: per_device(): lax.psum((mixer_gain_part, ffn_gain_part, out_bias_part, down_bias_part,...]
    dynamic_update_slice x32 -> x0, other arithmetic: 55.6 us -> none  [the longest x24 49.5 us: long_conv(): lax.scan(visit, jnp.zeros((channel_count, length), jnp.float32), jnp.aran...]
  transfers between devices with their start and end apart: 12 -> 0, of which waited for: 11 -> 0; matrix products, arithmetic and copies ran while one was open for 2% -> 0% of each run, Pallas kernels for 0% -> 0%
where the time goes in v2:
time: 212 us; the launch traced here: 211 us
  Pallas kernels  179 us (84%)
  local copies, waits for them, and re-layouts  26.5 us (12%)
  other arithmetic  4.2 us (2%)
    pallas_call x1, Pallas kernels, per_device(): pl.pallas_call(functools.partial(fused, sizes, names), out_shape=[jax.Sha...  179 us
    reshape x7, local copies, waits for them, and re-layouts, per_device(): row = lambda value: value.reshape(1, -1)  8.82 us
    unnamed x18, local copies, waits for them, and re-layouts  4.81 us

profile of v2, /device:TPU:0, one launch (start us, length us, event | category | flops | bytes accessed | tf_op | source)
XLA Modules:
  0.0 210.7 jit_solution(10640360114776844644)
XLA Ops:
  0.7 2.1 copy.53.refs_2_
  2.7 1.3 reshape.100.refs_9_
  4.0 1.3 reshape.108.refs_21_
  5.3 1.3 reshape.97.refs_6_
  6.5 1.3 reshape.98.refs_7_
  7.8 1.3 reshape.99.refs_8_
  9.1 1.2 reshape.101.refs_10_
  10.3 1.2 reshape.103.refs_13_
  11.5 179.3 %block.1 = (bf16[128,768]{1,0:T(8,128)(2,1)}, f32[128,768]{1,0:T(8,128)}, bf16[768,288]{1,0:T(8,128)(2,1)}, bf16[128,768]{1,0:T(8,128)(2,1)}, bf16[768,384]{1,0:...) custom-call(bf16[128,768]{1,0:T(8,128)(2,1)} %refs_0_.1, ...), custom_call_target="tpu_custom_call" | custom-call | tf_op jit(solution)/shard_map/block/pallas_call | solution.py:1179
  190.9 1.4 slice_bitcast_fusion.1
  192.3 1.7 slice_reduce_fusion
  194.0 1.4 slice.67
  195.3 1.3 slice.64
  196.7 1.3 slice_reduce_fusion.7
  198.0 1.0 slice_bitcast_fusion
  199.1 0.8 reshape.113
  199.9 0.8 slice_reduce_fusion.4
  201.9 1.3 slice_reduce_fusion.5
  203.8 1.2 slice_bitcast_fusion.5
  205.0 1.1 convert_element_type.14
  206.1 1.1 convert_element_type.15
  207.4 1.1 copy.55
  208.5 0.7 slice_convert_fusion
  209.9 0.7 copy.59
  (19 shorter events, 2.9 us)
Async XLA Ops:
  190.9 10.5 %copy-start.6 = (f32[8,288]{1,0:T(8,128)S(1)}, f32[8,288]{1,0:T(8,128)}, u32[]{:S(2)}) copy-start(f32[8,288]{1,0:T(8,128)} %get-tuple-element.39) | copy-start | bytes 27652
  190.9 14.2 %copy-start.1 = (bf16[768,384]{1,0:T(8,128)(2,1)S(1)}, bf16[768,384]{1,0:T(8,128)(2,1)}, u32[]{:S(2)}) copy-start(bf16[768,384]{1,0:T(8,128)(2,1)} %get-tuple-element.42) | copy-start | bytes 1769476
  199.1 7.0 %copy-start = (bf16[384,768]{1,0:T(8,128)(2,1)S(1)}, bf16[384,768]{1,0:T(8,128)(2,1)}, u32[]{:S(2)}) copy-start(bf16[384,768]{1,0:T(8,128)(2,1)} %get-tuple-element.43) | copy-start | bytes 1769476
  206.1 1.3 copy-start.2
  207.2 1.3 copy-start.5
  207.2 2.0 copy-start.4
  207.2 2.7 %copy-start.3 = (f32[128,768]{1,0:T(8,128)S(1)}, f32[128,768]{1,0:T(8,128)}, u32[]{:S(2)}) copy-start(f32[128,768]{1,0:T(8,128)} %get-tuple-element.123) | copy-start | bytes 1179652

commit v3 on v2

v3 whole, which is shorter than its diff:
```python
import functools
import math
import types

import jax
import jax.numpy as jnp
import numpy as np
from jax import lax
from jax.experimental import pallas as pl
from jax.experimental.pallas import tpu as pltpu
from jax.sharding import PartitionSpec as P

D = 768
BANDS = 16
EMB = 2 * BANDS + 1
FILT = 64
LONG = 1024
BLOCK = 256
BINS = 2 * BLOCK
COUNT = LONG // BLOCK
LANES = 128
WIDE = 3 * LANES
MESH = pl.DeviceIdType.MESH
BF16 = jnp.bfloat16
F32 = jnp.float32
EPS = 1e-05
ROOT = math.sqrt(2.0 / math.pi)
CUBE = 0.044715

PAY_VEC, PAY_PEN, PAY_HID, PAY_EMB, PAY_ROWS = 0, 18, 24, 88, 128
SHARD_DECAY, SHARD_PAR, SHARD_ROWS = 64, 72, 96


def wave_table(shift):
    bins = np.arange(BLOCK)[:, None]
    angle = np.pi * (2 * bins + 1) * (np.arange(BLOCK)[None, :] + shift) / BINS
    return np.concatenate([np.cos(angle), -np.sin(angle)], 0)


NEAR, FAR = wave_table(0), wave_table(-BLOCK)
WAVES = np.concatenate([NEAR, FAR], 1)
UNWAVES = np.concatenate([NEAR.T, FAR.T], 1) / BLOCK


def position_features():
    tau = np.arange(LONG) / LONG
    angles = 2.0 * np.pi * np.arange(1, BANDS + 1)[:, None] * tau[None, :]
    return np.concatenate([tau[None, :], np.cos(angles), np.sin(angles)], 0)


def dot(left, right, dims=((1,), (0,)), precision=None):
    return lax.dot_general(
        left, right, (dims, ((), ())), precision=precision, preferred_element_type=F32
    )


def dot_nt(left, right, precision=None):
    return dot(left, right, ((1,), (1,)), precision)


def dot_tn(left, right, precision=None):
    return dot(left, right, ((0,), (0,)), precision)


HIGH = lax.Precision.HIGHEST


def sin_cos(angle):
    turns = jnp.floor(angle * (2.0 / math.pi) + 0.5)
    rest = angle - turns * 1.5703125
    rest = rest - turns * 4.837512969970703125e-4
    rest = rest - turns * 7.54978995489188e-8
    square = rest * rest
    sine = rest + rest * square * (
        -1.6666654611e-1 + square * (8.3321608736e-3 + square * -1.9515295891e-4)
    )
    cosine = (
        1.0
        - 0.5 * square
        + square
        * square
        * (4.166664568298827e-2 + square * (-1.388731625493765e-3 + square * 2.443315711809948e-5))
    )
    half = jnp.floor(turns * 0.5)
    odd = turns - 2.0 * half
    sign = 1.0 - 2.0 * (half - 2.0 * jnp.floor(half * 0.5))
    swapped = odd > 0.5
    return (
        jnp.where(swapped, cosine, sine) * sign,
        jnp.where(swapped, -sine, cosine) * sign,
    )


def norm_parts(values):
    center = values - jnp.mean(values, axis=-1, keepdims=True)
    scale = lax.rsqrt(jnp.mean(center * center, axis=-1, keepdims=True) + EPS)
    return center * scale, scale


def norm_back(grad, gain, unit, scale):
    inner = grad * gain
    return scale * (
        inner
        - jnp.mean(inner, axis=-1, keepdims=True)
        - unit * jnp.mean(inner * unit, axis=-1, keepdims=True)
    )


def column(row):
    size = row.shape[1]
    same = lax.broadcasted_iota(jnp.int32, (size, size), 0) == lax.broadcasted_iota(
        jnp.int32, (size, size), 1
    )
    return jnp.sum(jnp.where(same, row, 0.0), axis=1, keepdims=True)


def fused(s, names, *refs):
    r = types.SimpleNamespace(**dict(zip(names, refs)))
    ranks, halves, inner, rows = s.ranks, s.halves, s.inner, s.rows
    channels, hidden = s.channels, s.hidden
    dp, mp = lax.axis_index("dp"), lax.axis_index("mp")
    y, c = dp // 2, dp % 2
    q, j = mp // halves, mp % halves
    other, across = 1 - c, 1 - q
    outer = halves // inner

    def device(yy, cc, qq, jj):
        return (yy * 2 + cc, qq * halves + jj)

    def ahead(k):
        return ((j // inner + k // inner) % outer) * inner + (j % inner + k % inner) % inner

    def behind(k):
        return ((j // inner + outer - k // inner) % outer) * inner + (
            j % inner + inner - k % inner
        ) % inner

    sibling = device(y, other, q, j)
    partner = device(y, other, across, j)
    moved = c != q

    def remote(src, dst, send, recv, target):
        return pltpu.make_async_remote_copy(
            src_ref=src,
            dst_ref=dst,
            send_sem=send,
            recv_sem=recv,
            device_id=target,
            device_id_type=MESH,
        )

    def block_rows(cc, jj):
        return pl.ds(pl.multiple_of((cc * halves + jj) * rows, rows), rows)

    mine = block_rows(c, j)

    barrier = pltpu.get_barrier_semaphore()
    greeted = [sibling, partner]
    for k in range(1, halves):
        greeted += [device(y, c, q, ahead(k)), device(y, other, q, ahead(k))]
    for dy in range(ranks):
        for dq in range(2):
            if dy or dq:
                greeted.append(device((y + dy) % ranks, c, (q + dq) % 2, j))
    for target in greeted:
        pl.semaphore_signal(barrier, inc=1, device_id=target, device_id_type=MESH)

    def load(name):
        i = s.loads.index(name)
        return pltpu.make_async_copy(
            getattr(r, name + "_any"), getattr(r, name), r.load_sem.at[i]
        )

    pl.semaphore_wait(barrier, len(greeted))

    par = r.par_own
    theirs = block_rows(other, j)
    x, own_par, w_in, grads, w_out, w_up, w_down = range(7)
    takes = [
        (r.x_any, r.x_in, r.x_in),
        (par, r.par_in, r.par_in),
        (r.win_any, r.win, r.win),
        (r.og_any, r.g_out.at[theirs], r.g_out.at[mine]),
        (r.wout_any, r.wout.at[pl.ds(0, channels)], r.wout.at[pl.ds(0, channels)]),
        (r.wup_any, r.wup, r.wup),
        (r.wdn_any, r.wdn, r.wdn),
    ]
    owner = jnp.logical_not(moved)

    def cut_rows(i, yy):
        size = takes[i][0].shape[0] // ranks
        return pl.ds(pl.multiple_of(yy * size, 16), size)

    def in_parts(i):
        return i in (w_in, w_up, w_down) and takes[i][0].shape[0] % (16 * ranks) == 0

    def take(i, arriving=False):
        src, dst, here = takes[i]
        dst = here if arriving else dst
        if in_parts(i):
            src, dst = src.at[cut_rows(i, y)], dst.at[cut_rows(i, y)]
        return remote(src, dst, r.take_send.at[i], r.take_recv.at[i], partner)

    def take_local(i):
        return pltpu.make_async_copy(takes[i][0], takes[i][2], r.take_local.at[i])

    def pass_copy(i, dy):
        at = takes[i][2].at[cut_rows(i, y)]
        return remote(
            at,
            at,
            r.cut_send.at[i, dy],
            r.cut_recv.at[i, dy],
            device((y + dy) % ranks, c, q, j),
        )

    def take_start(*which, after=()):
        @pl.when(moved)
        def _():
            for i in after:
                take(i).wait_send()
            for i in which:
                take(i).start()

    def take_pass(*which):
        @pl.when(moved)
        def _():
            for i in which:
                take(i, True).wait_recv()
                if in_parts(i):
                    for dy in range(1, ranks):
                        pass_copy(i, dy).start()

    def taken(*which):
        @pl.when(moved)
        def _():
            for i in which:
                if i not in (w_in, w_up, w_down):
                    take(i, True).wait_recv()
                elif in_parts(i):
                    for dy in range(1, ranks):
                        at = takes[i][2].at[cut_rows(i, (y + ranks - dy) % ranks)]
                        remote(
                            at,
                            at,
                            r.cut_send.at[i, dy],
                            r.cut_recv.at[i, dy],
                            device((y + ranks - dy) % ranks, c, q, j),
                        ).wait_recv()
                        pass_copy(i, dy).wait_send()

        @pl.when(owner)
        def _():
            for i in which:
                take_local(i).wait()

    take_start(x)
    @pl.when(owner)
    def _():
        for i in range(len(takes)):
            if i != own_par:
                take_local(i).start()

    for name in s.loads:
        load(name).start()
    for name in s.loads:
        if name not in s.late_loads:
            load(name).wait()

    def line(ref):
        return jnp.reshape(ref[...], (1, ref.shape[0]))

    par[...] = jnp.zeros_like(par)
    par[0:1, 0 : 3 * channels] = line(r.in_bias)
    par[1:4, 0 : 3 * channels] = r.short_taps[...]
    par[4:5, 0:channels] = line(r.skip_gain)
    par[5:6, 0:hidden] = line(r.up_bias).astype(F32)

    @pl.when(owner)
    def _():
        take_local(own_par).start()

    def seat(n, cc, jj):
        size = PAY_ROWS // (2 * halves) if n == 5 else SHARD_ROWS if n == 4 else rows
        return pl.ds(pl.multiple_of((cc * halves + jj) * size, size), size)

    def gather_copies(n, held):
        mine = seat(n, c, j)
        out = []
        for k in range(1, halves):
            out.append(
                remote(
                    held.at[mine],
                    held.at[mine],
                    r.gather_send.at[n, k],
                    r.gather_recv.at[n, k],
                    device(y, c, q, ahead(k)),
                )
            )
        out.append(
            remote(
                held.at[mine],
                held.at[mine],
                r.gather_send.at[n, 0],
                r.gather_recv.at[n, 0],
                sibling,
            )
        )
        return out

    def gather_start(n, held):
        for copy in gather_copies(n, held):
            copy.start()

    def gather_finish(n, held):
        forwards = []
        for k in range(1, halves):
            came = held.at[seat(n, c, behind(k))]
            remote(
                came,
                came,
                r.gather_send.at[n, k],
                r.gather_recv.at[n, k],
                device(y, c, q, behind(k)),
            ).wait_recv()
            forward = remote(
                came, came, r.hop_send.at[n, k], r.hop_recv.at[n, k], sibling
            )
            forward.start()
            forwards.append(forward)
        for k in range(halves):
            came = held.at[seat(n, other, behind(k))]
            recv = r.hop_recv.at[n, k] if k else r.gather_recv.at[n, 0]
            remote(came, came, r.hop_send.at[n, k], recv, sibling).wait_recv()
        for copy in gather_copies(n, held) + forwards:
            copy.wait_send()

    def first_norm():
        unit, _ = norm_parts(r.x_in[...].astype(F32))
        r.g_one[mine, :] = (unit * line(r.mixer_gain)).astype(BF16)
        gather_start(0, r.g_one)

    @pl.when(owner)
    def _():
        take_local(x).wait()
        first_norm()
        take_local(grads).wait()
        gather_start(1, r.g_out)

    pack = y * 2 + q
    segments = []
    for i in range(COUNT):
        found = jnp.int32(-1)
        for k in range(s.sequences):
            start = r.offsets[k]
            hit = (
                (r.owners[k] == pack)
                & (start <= i * BLOCK)
                & (start + r.lengths[k] > i * BLOCK)
            )
            found = jnp.where(hit, jnp.int32(k), found)
        segments.append(found)
    valid = [jnp.where(seg >= 0, jnp.float32(1), jnp.float32(0)) for seg in segments]
    joined = [
        [valid[i] * jnp.where(segments[i] == segments[p], jnp.float32(1), jnp.float32(0)) for p in range(i + 1)]
        for i in range(COUNT)
    ]
    follows = [jnp.float32(0)] + [joined[i][i - 1] for i in range(1, COUNT)]

    row_index = lax.broadcasted_iota(jnp.int32, (3 * channels, WIDE), 0)
    lane_index = lax.broadcasted_iota(jnp.int32, (3 * channels, WIDE), 1)
    within = lane_index % LANES
    order = jnp.where(
        (row_index == 3 * within + lane_index // LANES) & (within < channels), 1.0, 0.0
    )
    r.order[...] = order.astype(BF16)
    r.order_wide[...] = order

    load("features").wait()
    features = r.features[...]
    embed_freq, embed_bias = column(line(r.embed_freq)), column(line(r.embed_bias))
    hidden_freq, hidden_bias = column(line(r.hidden_freq)), column(line(r.hidden_bias))
    first_sum = dot_tn(r.embed_weight[...], features, HIGH) + embed_bias
    first, first_cos = sin_cos(embed_freq * first_sum)
    r.first_sum[...] = first_sum
    r.first[...] = first
    r.first_cos[...] = first_cos
    take_start(w_in, own_par, after=(x,))
    second_sum = dot_tn(r.hidden_weight[...], first, HIGH) + hidden_bias
    second, second_cos = sin_cos(hidden_freq * second_sum)
    r.second_sum[...] = second_sum
    r.second[...] = second
    r.second_cos[...] = second_cos
    half_rows = LONG // 2
    chunks = half_rows // BLOCK
    per_chunk = BLOCK // rows

    def half_chunk(cc, t):
        return pl.ds(pl.multiple_of(cc * half_rows + t * BLOCK, BLOCK), BLOCK)

    def chunk_rows(t):
        return pl.ds(pl.multiple_of(t * BLOCK, BLOCK), BLOCK)

    def place(jj):
        return pl.ds(pl.multiple_of(jj * rows, rows), rows)

    def chip_copy(n, t):
        return remote(
            r.chip_out.at[n, chunk_rows(t)],
            r.chip_in.at[n, chunk_rows(t)],
            r.chip_send.at[n, t],
            r.chip_recv.at[n, t],
            sibling,
        )

    def link_copy(n, jj):
        return remote(
            r.link_out.at[n, place(jj)],
            r.link_in.at[n, place(j)],
            r.link_send.at[n, jj],
            r.link_recv.at[n, j],
            device(y, c, q, jj),
        )

    def chip_give(n, t, value):
        r.chip_out[n, chunk_rows(t), :] = value.astype(BF16)
        chip_copy(n, t).start()

    def chip_add(n, t, value):
        chip_copy(n, t).wait_recv()
        r.link_out[n, chunk_rows(t), :] = (
            value + r.chip_in[n, chunk_rows(t), :].astype(F32)
        ).astype(BF16)

    def link_start(n, t):
        for i in range(per_chunk):
            jj = t * per_chunk + i

            @pl.when(jj != j)
            def _():
                link_copy(n, jj).start()

    def scatter(n, part):
        def give(t, carry):
            chip_give(n, t, part(half_chunk(other, t)))
            return carry

        lax.fori_loop(0, chunks, give, 0)

        def send(t, carry):
            chip_add(n, t, part(half_chunk(c, t)))
            link_start(n, t)
            return carry

        lax.fori_loop(0, chunks, send, 0)

    def scatter_finish(n):
        total = r.link_out[n, place(j), :].astype(F32)
        for k in range(1, halves):
            jj = behind(k)
            came = r.link_in.at[n, place(jj)]
            remote(
                came, came, r.link_send.at[n, jj], r.link_recv.at[n, jj], device(y, c, q, jj)
            ).wait_recv()
            total = total + r.link_in[n, place(jj), :].astype(F32)
        for t in range(chunks):
            chip_copy(n, t).wait_send()
        for k in range(1, halves):
            link_copy(n, ahead(k)).wait_send()
        return total

    @pl.when(moved)
    def _():
        take(x, True).wait_recv()
        first_norm()

    shard = c * halves + j
    pick_row = lax.broadcasted_iota(jnp.int32, (D, LANES), 0)
    pick_lane = lax.broadcasted_iota(jnp.int32, (D, LANES), 1)
    pick = jnp.where((pick_row == shard * channels + pick_lane) & (pick_lane < channels), 1.0, 0.0)
    own_filter = dot(r.filter_weight[...], pick, precision=HIGH)
    own_decay = dot(jnp.broadcast_to(line(r.decay_rate), (8, D)), pick, precision=HIGH)[0:1]
    r.own_filter[...] = own_filter
    r.own_decay[...] = jnp.broadcast_to(own_decay, (8, LANES))
    r.spread[...] = jnp.zeros_like(r.spread)
    for i in range(COUNT):
        at = slice(i * BLOCK, (i + 1) * BLOCK)
        tau = (
            lax.broadcasted_iota(jnp.int32, (BLOCK, LANES), 0) + i * BLOCK
        ).astype(F32) * (1.0 / LONG)
        kernel = dot_tn(second[:, at], own_filter, HIGH) * jnp.exp(-tau * own_decay)
        r.kernel[at, :] = kernel
        low = kernel.astype(BF16)
        r.spread[0:BLOCK, i * LANES : (i + 1) * LANES] = low
        if i + 1 < COUNT:
            r.spread[BLOCK:BINS, (i + 1) * LANES : (i + 2) * LANES] = low
    take_start(grads, w_out, after=(w_in, own_par))
    take_pass(w_in)
    load("waves").wait()
    load("unwaves").wait()
    r.kernel_wave[...] = dot(r.waves[...], r.spread[...])
    gather_finish(0, r.g_one)

    @pl.when(moved)
    def _():
        take(grads, True).wait_recv()
        gather_start(1, r.g_out)

    take_start(w_up, w_down, after=(grads,))
    taken(own_par, w_in)
    par_wide = dot(r.par_in[:, 0 : 3 * channels], r.order_wide[...], precision=HIGH)
    r.taps[...] = par_wide
    r.win_apart[...] = dot_tn(r.order[...], r.win[...]).astype(BF16)
    r.wout[channels:, :] = jnp.zeros_like(r.wout[channels:, :])

    def project(i, carry):
        at = pl.ds(pl.multiple_of(i * BINS, BINS), BINS)
        r.projected[at, :] = dot_nt(r.g_one[at, :], r.win_apart[...]) + r.taps[0:1, :]
        return carry

    lax.fori_loop(0, LONG // BINS, project, 0)

    rows_here = lax.broadcasted_iota(jnp.int32, (BLOCK, 1), 0)

    def back_rows(i):
        now = r.projected[i * BLOCK : (i + 1) * BLOCK, :]
        one, two = pltpu.roll(now, 1, 0), pltpu.roll(now, 2, 0)
        if i:
            edge = r.projected[i * BLOCK - 8 : i * BLOCK, :] * follows[i]
            last, before = edge[7:8], edge[6:7]
        else:
            last = before = jnp.zeros((1, WIDE), F32)
        one = jnp.where(rows_here == 0, last, one)
        two = jnp.where(rows_here == 0, before, jnp.where(rows_here == 1, last, two))
        return now, one, two

    for i in range(COUNT):
        now, one, two = back_rows(i)
        short = r.taps[1:2, :] * now + r.taps[2:3, :] * one + r.taps[3:4, :] * two
        r.short[i * BLOCK : (i + 1) * BLOCK, :] = short
        signal = short[:, 2 * LANES :] * short[:, LANES : 2 * LANES] * valid[i]
        r.signal[:, i * LANES : (i + 1) * LANES] = signal.astype(BF16)

    near = r.waves[:, 0:BLOCK]
    unnear = r.unwaves[:, 0:BINS]
    r.signal_wave[...] = dot(near, r.signal[...])
    step = 16

    def load_wave(ref, at, count=COUNT):
        low, high = pl.ds(at, step), pl.ds(at + BLOCK, step)
        return [
            (ref[low, i * LANES : (i + 1) * LANES], ref[high, i * LANES : (i + 1) * LANES])
            for i in range(count)
        ]

    def store_wave(ref, base, at, i, pair):
        ref[pl.ds(base + at, step), i * LANES : (i + 1) * LANES] = pair[0].astype(BF16)
        ref[pl.ds(base + at + BLOCK, step), i * LANES : (i + 1) * LANES] = pair[1].astype(BF16)

    def weighted(terms):
        real = imag = None
        for weight, (a, b) in terms:
            real = a * weight if real is None else real + a * weight
            imag = b * weight if imag is None else imag + b * weight
        return real, imag

    def times(left, right):
        return left[0] * right[0] - left[1] * right[1], left[0] * right[1] + left[1] * right[0]

    def times_conj(left, right):
        return left[0] * right[0] + left[1] * right[1], left[0] * right[1] - left[1] * right[0]

    def forward_wave(n, carry):
        at = pl.multiple_of(n * step, step)
        kernels, signals = load_wave(r.kernel_wave, at), load_wave(r.signal_wave, at)
        for i in range(COUNT):
            store_wave(
                r.product,
                0,
                at,
                i,
                weighted([(joined[i][p], times(kernels[i - p], signals[p])) for p in range(i + 1)]),
            )
        return carry

    lax.fori_loop(0, BLOCK // step, forward_wave, 0)
    skip = r.par_in[4:5, 0:LANES]
    convolved = dot(unnear, r.product[0:BINS, :])
    for i in range(COUNT):
        at = slice(i * BLOCK, (i + 1) * BLOCK)
        lanes = slice(i * LANES, (i + 1) * LANES)
        direct = convolved[:, lanes] + skip * r.signal[:, lanes].astype(F32)
        r.direct[at, :] = direct
        r.mixed[at, :] = (direct * r.short[at, 0:LANES]).astype(BF16)

    taken(w_out)
    scatter(0, lambda at: dot(r.mixed[at, :], r.wout[...]))
    take_pass(w_up)
    middle = r.x_in[...].astype(F32) + line(r.out_bias) + scatter_finish(0)
    unit, scale = norm_parts(middle)
    r.g_two[mine, :] = (unit * line(r.ffn_gain)).astype(BF16)
    gather_start(2, r.g_two)
    r.middle[...] = middle
    r.unit[...] = unit
    r.scale[...] = jnp.broadcast_to(scale, r.scale.shape)
    take_pass(w_down)
    gather_finish(1, r.g_out)
    gather_finish(2, r.g_two)
    taken(w_up, w_down)

    def feed(at):
        value = dot(r.g_two[at, :], r.wup[...]) + r.par_in[5:6, 0:hidden]
        square = value * value
        bend = jnp.tanh(ROOT * value * (1.0 + CUBE * square))
        half = 0.5 * (1.0 + bend)
        active = (value * half).astype(BF16)
        slope = half + 0.5 * value * (1.0 - bend * bend) * (ROOT * (1.0 + 3.0 * CUBE * square))
        grad = (slope * dot_nt(r.g_out[at, :], r.wdn[...])).astype(BF16)
        r.active[at, :] = active
        r.hidden_grad[at, :] = grad
        return dot_nt(grad, r.wup[...]), dot(active, r.wdn[...])

    def feed_step(i, carry):
        t, own = i // 2, i % 2
        back, forth = feed(half_chunk(own * c + (1 - own) * other, t))

        @pl.when(own == 0)
        def _():
            chip_give(1, t, back)
            chip_give(2, t, forth)

        @pl.when(own == 1)
        def _():
            chip_add(1, t, back)
            link_start(1, t)
            chip_add(2, t, forth)

        return carry

    lax.fori_loop(0, 2 * chunks, feed_step, 0)

    sums = [
        (r.grad_in, r.part_in, r.y_in, r.z_in, r.gwin),
        (r.grad_out, r.part_out, r.y_out, r.z_out, r.gwout),
        (r.grad_up, r.part_up, r.y_up, r.z_up, r.gwup),
        (r.grad_dn, r.part_dn, r.y_dn, r.z_dn, r.gwdn),
    ]
    def part_rows(ref, yy):
        size = ref.shape[0] // ranks
        return pl.ds(pl.multiple_of(yy * size, 16), size)

    def y_copy(w, dy):
        full, _, came, _, _ = sums[w]
        to = (y + dy) % ranks
        return remote(
            full.at[part_rows(full, to)],
            came.at[dy],
            r.y_send.at[w, dy],
            r.y_recv.at[w, dy],
            device(to, c, q, j),
        )

    def z_copy(w):
        _, part, _, came, _ = sums[w]
        return remote(
            part, came, r.z_send.at[w], r.z_recv.at[w], device(y, c, across, j)
        )

    def out_copy(w, dy):
        final = sums[w][4]
        at = part_rows(final, y)
        return remote(
            final.at[at],
            final.at[at],
            r.out_send.at[w, dy],
            r.out_recv.at[w, dy],
            device((y + dy) % ranks, c, q, j),
        )

    def chip_final(w, dy):
        final = sums[w][4]
        at = part_rows(final, (y + ranks - dy) % ranks)
        return remote(
            final.at[at],
            final.at[at],
            r.fin_send.at[w, dy],
            r.fin_recv.at[w, dy],
            sibling,
        )

    def sum_start(w):
        for dy in range(1, ranks):
            y_copy(w, dy).start()

    def sum_cross(w):
        full, part, came, _, _ = sums[w]
        total = full[part_rows(full, y), :].astype(F32)
        for dy in range(1, ranks):
            y_copy(w, dy).wait_recv()
            total = total + came[dy].astype(F32)
        part[...] = total.astype(BF16)

        @pl.when(moved)
        def _():
            z_copy(w).start()

    def sum_close(w):
        _, part, _, came, final = sums[w]

        @pl.when(owner)
        def _():
            z_copy(w).wait_recv()
            final[part_rows(final, y), :] = (
                part[...].astype(F32) + came[...].astype(F32)
            ).astype(BF16)
            for dy in range(1, ranks):
                out_copy(w, dy).start()
            chip_final(w, 0).start()

    def sum_finish(w):
        final = sums[w][4]

        @pl.when(owner)
        def _():
            for dy in range(1, ranks):
                at = part_rows(final, (y + ranks - dy) % ranks)
                remote(
                    final.at[at],
                    final.at[at],
                    r.out_send.at[w, dy],
                    r.out_recv.at[w, dy],
                    sibling,
                ).wait_recv()
                chip_final(w, dy).start()
            for dy in range(1, ranks):
                out_copy(w, dy).wait_send()
            for dy in range(ranks):
                chip_final(w, dy).wait_send()

        @pl.when(moved)
        def _():
            for dy in range(ranks):
                chip_final(w, dy).wait_recv()
            z_copy(w).wait_send()

        for dy in range(1, ranks):
            y_copy(w, dy).wait_send()

    def weight_grad(target, left, right, by_right=False):
        def chunk(i, carry):
            at = pl.ds(pl.multiple_of(i * BLOCK, BLOCK), BLOCK)
            if by_right:
                target[0 : left.shape[1], at] = dot_tn(left[...], right[:, at]).astype(BF16)
            else:
                target[at, :] = dot_tn(left[:, at], right[...]).astype(BF16)
            return carry

        lax.fori_loop(0, D // BLOCK, chunk, 0)

    for grad, size in ((r.grad_dn, hidden), (r.grad_in, 3 * channels)):
        if grad.shape[0] > size:
            grad[size:, :] = jnp.zeros_like(grad[size:, :])
    weight_grad(r.grad_dn, r.active, r.g_out, True)
    sum_start(3)
    weight_grad(r.grad_up, r.g_two, r.hidden_grad)
    sum_start(2)

    seed = r.g_out[mine, :].astype(F32)
    ffn_back = scatter_finish(1)
    unit, scale = r.unit[...], jnp.concatenate([r.scale[...]] * (D // LANES), axis=1)
    middle_grad = seed + norm_back(ffn_back, line(r.ffn_gain), unit, scale)
    r.middle_grad[...] = middle_grad
    branch_grad = middle_grad.astype(BF16)
    r.g_back[mine, :] = branch_grad
    gather_start(3, r.g_back)
    vectors = [
        jnp.sum(ffn_back * unit, axis=0, keepdims=True),
        jnp.sum(branch_grad.astype(F32), axis=0, keepdims=True),
        jnp.sum(seed, axis=0, keepdims=True),
    ]
    r.pay[...] = jnp.zeros_like(r.pay)
    for v, vector in enumerate(vectors):
        for k in range(D // LANES):
            at = PAY_VEC + v * (D // LANES) + k
            r.pay[at : at + 1, :] = vector[:, k * LANES : (k + 1) * LANES]
    par_grad = r.par_grad
    par_grad[...] = jnp.zeros_like(par_grad)
    par_grad[5:6, 0:hidden] = jnp.sum(r.hidden_grad[...].astype(F32), axis=0, keepdims=True)
    sum_cross(3)
    sum_cross(2)
    gather_finish(3, r.g_back)
    for t in range(chunks):
        link_start(2, t)
    r.grad_out[...] = dot_tn(r.mixed[...], r.g_back[...]).astype(BF16)
    sum_start(1)

    skip_total = jnp.zeros((1, LANES), F32)
    for i in range(COUNT):
        at = slice(i * BLOCK, (i + 1) * BLOCK)
        lanes = slice(i * LANES, (i + 1) * LANES)
        mixed_grad = dot_nt(r.g_back[at, :], r.wout[...])
        r.short_grad[at, 0:LANES] = mixed_grad * r.direct[at, :]
        direct_grad = mixed_grad * r.short[at, 0:LANES]
        r.direct[at, :] = direct_grad
        r.direct_low[:, lanes] = direct_grad.astype(BF16)
        skip_total += jnp.sum(
            direct_grad * r.signal[:, lanes].astype(F32), axis=0, keepdims=True
        )
    par_grad[4:5, 0:LANES] = skip_total
    r.grad_wave[...] = dot(near, r.direct_low[...])
    r.back_product[...] = jnp.zeros_like(r.back_product)

    def backward_wave(n, carry):
        at = pl.multiple_of(n * step, step)
        kernels, signals = load_wave(r.kernel_wave, at), load_wave(r.signal_wave, at)
        grads = load_wave(r.grad_wave, at)
        for p in range(COUNT):
            terms = [(joined[i][p], times_conj(kernels[i - p], grads[i])) for i in range(p, COUNT)]
            store_wave(r.product, 0, at, p, weighted(terms))
        for d in range(COUNT):
            terms = [
                (joined[i][i - d], times_conj(signals[i - d], grads[i])) for i in range(d, COUNT)
            ]
            pair = weighted(terms)
            store_wave(r.back_product, 0, at, d, pair)
            if d:
                store_wave(r.back_product, BINS, at, d - 1, pair)
        return carry

    lax.fori_loop(0, BLOCK // step, backward_wave, 0)
    signal_grads = dot(unnear, r.product[0:BINS, :])
    for i in range(COUNT):
        at = slice(i * BLOCK, (i + 1) * BLOCK)
        lanes = slice(i * LANES, (i + 1) * LANES)
        signal_grad = (signal_grads[:, lanes] + skip * r.direct[at, :]) * valid[i]
        r.short_grad[at, LANES : 2 * LANES] = signal_grad * r.short[at, 2 * LANES :]
        r.short_grad[at, 2 * LANES :] = signal_grad * r.short[at, LANES : 2 * LANES]

    bias_total = jnp.zeros((1, WIDE), F32)
    tap_totals = [jnp.zeros((1, WIDE), F32) for _ in range(3)]
    for i in range(COUNT):
        at = slice(i * BLOCK, (i + 1) * BLOCK)
        now, one, two = back_rows(i)
        grad = r.short_grad[at, :]
        for t, value in enumerate((now, one, two)):
            tap_totals[t] += jnp.sum(grad * value, axis=0, keepdims=True)
        next_one = pltpu.roll(grad, BLOCK - 1, 0)
        next_two = pltpu.roll(grad, BLOCK - 2, 0)
        if i + 1 < COUNT:
            edge = r.short_grad[(i + 1) * BLOCK : (i + 1) * BLOCK + 8, :] * follows[i + 1]
            head, after = edge[0:1], edge[1:2]
        else:
            head = after = jnp.zeros((1, WIDE), F32)
        next_one = jnp.where(rows_here == BLOCK - 1, head, next_one)
        next_two = jnp.where(
            rows_here == BLOCK - 2, head, jnp.where(rows_here == BLOCK - 1, after, next_two)
        )
        low = (
            r.taps[1:2, :] * grad + r.taps[2:3, :] * next_one + r.taps[3:4, :] * next_two
        ).astype(BF16)
        bias_total += jnp.sum(low.astype(F32), axis=0, keepdims=True)
        r.projected_grad[at, :] = dot_nt(low, r.order[...]).astype(BF16)
    par_grad[0:1, :] = bias_total
    for t in range(3):
        par_grad[t + 1 : t + 2, :] = tap_totals[t]

    sum_cross(1)
    scatter(3, lambda at: dot(r.projected_grad[at, :], r.win[...]))

    weight_grad(r.grad_in, r.projected_grad, r.g_one, True)
    sum_start(0)

    kernel_grads = dot(r.unwaves[...], r.back_product[...])
    decay_total = jnp.zeros((1, LANES), F32)
    penalty = jnp.zeros((1, LANES), F32)
    own_filter = r.own_filter[...]
    own_decay = r.own_decay[0:1, :]
    lead = jnp.where(pack == 0, 1.0 / D, 0.0).astype(F32)
    for i in range(COUNT):
        at = slice(i * BLOCK, (i + 1) * BLOCK)
        tau = (
            lax.broadcasted_iota(jnp.int32, (BLOCK, LANES), 0) + i * BLOCK
        ).astype(F32) * (1.0 / LONG)
        kernel = r.kernel[at, :]
        weighed = tau * kernel
        penalty += jnp.sum(weighed * kernel, axis=0, keepdims=True) * lead
        kernel_grad = (
            kernel_grads[:, i * LANES : (i + 1) * LANES] + weighed * (2.0 * lead)
        )
        decay_total -= jnp.sum(kernel_grad * weighed, axis=0, keepdims=True)
        r.raw_grad[at, :] = kernel_grad * jnp.exp(-tau * own_decay)
    sums_y, sums_q = r.shard_y, r.shard_q
    sums_y[y] = jnp.zeros((SHARD_ROWS, LANES), F32)
    sums_y[y, 0:FILT, :] = dot(r.second[...], r.raw_grad[...], precision=HIGH)
    sums_y[y, SHARD_DECAY : SHARD_DECAY + 1, :] = decay_total
    for k in range(3):
        at = SHARD_PAR + 8 * k
        sums_y[y, at : at + 8, :] = par_grad[:, k * LANES : (k + 1) * LANES]

    def shard_y(dy, back=False):
        at = sums_y.at[(y + ranks - dy) % ranks if back else y]
        return remote(
            at, at, r.sy_send.at[dy], r.sy_recv.at[dy], device((y + dy) % ranks, c, q, j)
        )

    def shard_q(back=False):
        at = sums_q.at[across if back else q]
        return remote(at, at, r.sq_send.at[0], r.sq_recv.at[0], device(y, c, across, j))

    for dy in range(1, ranks):
        shard_y(dy).start()
    r.pay[PAY_PEN : PAY_PEN + 1, :] = penalty
    second_grad = dot_nt(own_filter, r.raw_grad[...], HIGH)
    angle_grad = second_grad * r.second_cos[...]
    freq_grad = jnp.sum(angle_grad * r.second_sum[...], axis=1, keepdims=True)
    sum_grad = angle_grad * column(line(r.hidden_freq))
    at = slice(PAY_HID, PAY_HID + FILT)
    r.pay[at, 0:FILT] = dot_nt(r.first[...], sum_grad, HIGH)
    r.pay[at, FILT : FILT + 1] = freq_grad
    r.pay[at, FILT + 1 : FILT + 2] = jnp.sum(sum_grad, axis=1, keepdims=True)
    angle_grad = dot(r.hidden_weight[...], sum_grad, precision=HIGH) * r.first_cos[...]
    r.pay[at, FILT + 2 : FILT + 3] = jnp.sum(
        angle_grad * r.first_sum[...], axis=1, keepdims=True
    )
    sum_grad = angle_grad * column(line(r.embed_freq))
    r.pay[at, FILT + 3 : FILT + 4] = jnp.sum(sum_grad, axis=1, keepdims=True)
    r.pay[PAY_EMB : PAY_EMB + EMB, 0:FILT] = dot_nt(features, sum_grad, HIGH)

    half_pay = PAY_ROWS // 2
    part_pay = half_pay // halves
    slot = y * 2 + q

    def pay_half(cc):
        return pl.ds(pl.multiple_of(cc * half_pay, half_pay), half_pay)

    def pay_chip():
        return remote(
            r.pay.at[pay_half(other)], r.pay_in, r.pay_send.at[0], r.pay_recv.at[0], sibling
        )

    def pay_link(jj):
        at = pl.ds(pl.multiple_of(jj * part_pay, part_pay), part_pay)
        return remote(
            r.pay_sum.at[at],
            r.pay_held.at[j],
            r.paylink_send.at[jj],
            r.paylink_recv.at[j],
            device(y, c, q, jj),
        )

    def slots_copies(n, held):
        out = []
        for dy in range(ranks):
            for dq in range(2):
                if dy or dq:
                    out.append(
                        remote(
                            held.at[slot],
                            held.at[slot],
                            r.cross_send.at[n, dy * 2 + dq],
                            r.cross_recv.at[n, dy * 2 + dq],
                            device((y + dy) % ranks, c, (q + dq) % 2, j),
                        )
                    )
        return out

    def slots_sum(n, held):
        for dy in range(ranks):
            for dq in range(2):
                if dy or dq:
                    yy, qq = (y + ranks - dy) % ranks, (q + dq) % 2
                    came = held.at[yy * 2 + qq]
                    remote(
                        came,
                        came,
                        r.cross_send.at[n, dy * 2 + dq],
                        r.cross_recv.at[n, dy * 2 + dq],
                        device(yy, c, qq, j),
                    ).wait_recv()
        return added(held, 2 * ranks)

    def added(held, count):
        total = held[0]
        for i in range(1, count):
            total = total + held[i]
        return total

    pay_chip().start()
    for w in (3, 2, 1):
        sum_close(w)

    pay_chip().wait_recv()
    r.pay_sum[...] = r.pay[pay_half(c), :] + r.pay_in[...]
    for k in range(1, halves):
        pay_link(ahead(k)).start()
    r.pay_held[j] = r.pay_sum[pl.ds(pl.multiple_of(j * part_pay, part_pay), part_pay), :]
    for dy in range(1, ranks):
        shard_y(dy, True).wait_recv()
    sums_q[q] = added(sums_y, ranks)
    shard_q().start()
    sum_cross(0)

    r.block_out[...] = (r.middle[...] + line(r.down_bias) + scatter_finish(2)).astype(BF16)
    gives = [(r.input_grad, r.input_any), (r.block_out, r.block_any)]

    def give(i):
        src, dst = gives[i]
        return remote(src, dst, r.give_send.at[i], r.give_recv.at[i], partner)

    def give_local(i):
        src, dst = gives[i]
        return pltpu.make_async_copy(src, dst, r.give_local.at[i])

    def give_start(i):
        @pl.when(moved)
        def _():
            give(i).start()

        @pl.when(owner)
        def _():
            give_local(i).start()

    give_start(1)

    for k in range(1, halves):
        jj = behind(k)
        remote(
            r.pay_held.at[jj],
            r.pay_held.at[jj],
            r.paylink_send.at[jj],
            r.paylink_recv.at[jj],
            device(y, c, q, jj),
        ).wait_recv()
    r.pay_cross[slot] = added(r.pay_held, halves)
    for copy in slots_copies(0, r.pay_cross):
        copy.start()
    shard_q(True).wait_recv()
    r.shards[pl.ds(pl.multiple_of(shard * SHARD_ROWS, SHARD_ROWS), SHARD_ROWS), :] = added(
        sums_q, 2
    )
    gather_start(4, r.shards)

    unit, scale = norm_parts(r.x_in[...].astype(F32))
    mixer_back = scatter_finish(3)
    r.input_grad[...] = (
        r.middle_grad[...] + norm_back(mixer_back, line(r.mixer_gain), unit, scale)
    ).astype(BF16)
    give_start(0)
    gain_row = jnp.sum(mixer_back * unit, axis=0, keepdims=True)
    r.late[...] = jnp.zeros_like(r.late)
    for k in range(D // LANES):
        r.late[k : k + 1, :] = gain_row[:, k * LANES : (k + 1) * LANES]

    def late_chip():
        return remote(r.late, r.late_in, r.late_send.at[0], r.late_recv.at[0], sibling)

    def late_links():
        return [
            remote(
                r.late_held.at[j],
                r.late_held.at[j],
                r.late_send.at[k],
                r.late_recv.at[k],
                device(y, c, q, ahead(k)),
            )
            for k in range(1, halves)
        ]

    late_chip().start()

    def store(name):
        i = s.stores.index(name)
        return pltpu.make_async_copy(
            getattr(r, name), getattr(r, name + "_out"), r.store_sem.at[i]
        )

    r.pay_total[seat(5, c, j), :] = slots_sum(0, r.pay_cross)
    gather_start(5, r.pay_total)
    late_chip().wait_recv()
    r.late_held[j] = r.late[...] + r.late_in[...]
    for copy in late_links():
        copy.start()
    sum_close(0)
    for k in range(1, halves):
        came = r.late_held.at[behind(k)]
        remote(
            came, came, r.late_send.at[k], r.late_recv.at[k], device(y, c, q, behind(k))
        ).wait_recv()
    r.late_cross[slot] = added(r.late_held, halves)
    for copy in slots_copies(1, r.late_cross):
        copy.start()

    gather_finish(4, r.shards)
    store("shards").start()
    home = pl.multiple_of((q * halves + j) * SHARD_ROWS, SHARD_ROWS)
    wide = jnp.concatenate(
        [r.shards[pl.ds(home + SHARD_PAR + 8 * k, 8), :] for k in range(3)], axis=1
    )
    r.par_wide[...] = wide
    r.par_close[...] = dot_nt(wide, r.order_wide[...], HIGH)
    store("par_wide").start()
    store("par_close").start()
    for w, name in ((3, "gwdn"), (2, "gwup"), (1, "gwout")):
        sum_finish(w)
        store(name).start()
    gather_finish(5, r.pay_total)
    store("pay_total").start()
    r.late_total[...] = slots_sum(1, r.late_cross)
    store("late_total").start()
    sum_finish(0)
    store("gwin").start()
    for name in s.stores:
        store(name).wait()

    pay_chip().wait_send()
    for k in range(1, halves):
        pay_link(ahead(k)).wait_send()
    for dy in range(1, ranks):
        shard_y(dy).wait_send()
    shard_q().wait_send()
    late_chip().wait_send()
    for copy in late_links() + slots_copies(0, r.pay_cross) + slots_copies(1, r.late_cross):
        copy.wait_send()

    @pl.when(moved)
    def _():
        for i in (w_out, w_up, w_down):
            take(i).wait_send()
        for i in range(len(gives)):
            give(i).wait()

    @pl.when(owner)
    def _():
        for i in range(len(gives)):
            give_local(i).wait()


def close(s, names, *refs):
    r = types.SimpleNamespace(**dict(zip(names, refs)))
    lines = D // LANES

    def load(name):
        i = s.loads.index(name)
        return pltpu.make_async_copy(
            getattr(r, name + "_any"), getattr(r, name), r.load_sem.at[i]
        )

    def store(name):
        i = s.stores.index(name)
        return pltpu.make_async_copy(getattr(r, name), getattr(r, name + "_out"), r.store_sem.at[i])

    def put(**values):
        for name, value in values.items():
            held = getattr(r, name)
            held[...] = value if value.shape == held.shape else jnp.reshape(value, held.shape)
            store(name).start()

    for name in s.loads:
        load(name).start()
    load("block").wait()
    through = pltpu.make_async_copy(r.block, r.block_out, r.block_sem)
    through.start()
    for name in ("gwin", "gwup", "gwdn", "gwout", "input"):
        load(name).wait()
        held = getattr(r, name)
        size = getattr(r, name + "_wide").shape[0]
        put(**{name + "_wide": held[0:size, :].astype(F32)})
    load("pay_total").wait()
    pay = r.pay_total

    def long_row(ref, at):
        return jnp.concatenate([ref[at + k : at + k + 1, :] for k in range(lines)], axis=1)

    same = lax.broadcasted_iota(jnp.int32, (FILT, FILT), 0) == lax.broadcasted_iota(
        jnp.int32, (FILT, FILT), 1
    )

    def vector_of(k):
        col = pay[PAY_HID : PAY_HID + FILT, FILT + k : FILT + k + 1]
        return jnp.sum(jnp.where(same, col, 0.0), axis=0, keepdims=True)

    put(ffn_gain=long_row(pay, PAY_VEC))
    put(out_bias=long_row(pay, PAY_VEC + lines))
    put(down_bias=long_row(pay, PAY_VEC + 2 * lines))
    put(embed_weight=pay[PAY_EMB : PAY_EMB + EMB, 0:FILT])
    put(embed_bias=vector_of(3))
    put(embed_freq=vector_of(2))
    put(hidden_weight=pay[PAY_HID : PAY_HID + FILT, 0:FILT])
    put(hidden_bias=vector_of(1))
    put(hidden_freq=vector_of(0))
    r.penalty_out[0] = jnp.sum(pay[PAY_PEN : PAY_PEN + 1, :])
    load("late_total").wait()
    put(mixer_gain=long_row(r.late_total, 0))
    load("par_wide").wait()
    load("par_close").wait()
    put(in_bias=r.par_close[0:1, :])
    put(short_taps=r.par_close[1:4, :])
    put(skip_gain=r.par_wide[4:5, 0 : s.channels])
    put(up_bias=r.par_wide[5:6, 0 : s.hidden])
    load("shards").wait()
    for i in range(2 * s.halves):
        at = slice(i * s.channels, (i + 1) * s.channels)
        base = i * SHARD_ROWS
        r.filter_weight[:, at] = r.shards[base : base + FILT, 0 : s.channels]
        r.decay_row[0:1, at] = r.shards[
            base + SHARD_DECAY : base + SHARD_DECAY + 1, 0 : s.channels
        ]
    store("filter_weight").start()
    put(decay_rate=r.decay_row[0:1, :])
    for name in s.stores:
        store(name).wait()
    through.wait()


def round_up(value, unit):
    return (value + unit - 1) // unit * unit


def solution(mesh):
    n_dp, n_mp = mesh.shape["dp"], mesh.shape["mp"]

    def per_device(
        block_input,
        mixer_gain,
        in_weight,
        in_bias,
        short_taps,
        skip_gain,
        out_weight,
        out_bias,
        ffn_gain,
        up_weight,
        up_bias,
        down_weight,
        down_bias,
        embed_weight,
        embed_bias,
        embed_freq,
        hidden_weight,
        hidden_bias,
        hidden_freq,
        filter_weight,
        decay_rate,
        out_grad,
        sequence_lengths,
        sequence_rank,
        sequence_offset,
    ):
        ranks, halves = n_dp // 2, n_mp // 2
        rows = block_input.shape[0]
        channels, hidden = skip_gain.shape[0], up_weight.shape[1]
        down_rows = round_up(hidden, 16 * ranks)
        in_rows = round_up(3 * channels, 16 * ranks)
        group = 2 * halves
        anywhere = pl.BlockSpec(memory_space=pl.ANY)
        scalar = pl.BlockSpec(memory_space=pltpu.SMEM)
        small = dict(
            mixer_gain=mixer_gain,
            ffn_gain=ffn_gain,
            out_bias=out_bias,
            down_bias=down_bias,
            in_bias=in_bias,
            short_taps=short_taps,
            skip_gain=skip_gain,
            embed_weight=embed_weight,
            embed_bias=embed_bias,
            embed_freq=embed_freq,
            hidden_weight=hidden_weight,
            hidden_bias=hidden_bias,
            hidden_freq=hidden_freq,
            filter_weight=filter_weight,
            decay_rate=decay_rate,
            features=jnp.asarray(position_features(), F32),
            waves=jnp.asarray(WAVES, BF16),
            unwaves=jnp.asarray(UNWAVES, BF16),
        )
        inputs = dict(
            x_any=(block_input, anywhere),
            og_any=(out_grad, anywhere),
            win_any=(in_weight.T, anywhere),
            wout_any=(out_weight, anywhere),
            wup_any=(up_weight, anywhere),
            wdn_any=(down_weight, anywhere),
            up_bias=(up_bias, pl.BlockSpec(memory_space=pltpu.VMEM)),
            lengths=(sequence_lengths, scalar),
            owners=(sequence_rank, scalar),
            offsets=(sequence_offset, scalar),
        )
        for name, value in small.items():
            inputs[name + "_any"] = (value, anywhere)
        kept = dict(
            gwin=((in_rows, D), BF16),
            gwout=((LANES, D), BF16),
            gwup=((D, hidden), BF16),
            gwdn=((down_rows, D), BF16),
            pay_total=((PAY_ROWS, LANES), F32),
            late_total=((8, LANES), F32),
            shards=((group * SHARD_ROWS, LANES), F32),
            par_wide=((8, WIDE), F32),
            par_close=((8, 3 * channels), F32),
        )
        outputs = dict(block_any=((rows, D), BF16), input_any=((rows, D), BF16))
        for name, kind in kept.items():
            outputs[name + "_out"] = kind
        sizes = types.SimpleNamespace(
            ranks=ranks,
            halves=halves,
            inner=n_mp // 4,
            rows=rows,
            channels=channels,
            hidden=hidden,
            sequences=sequence_lengths.shape[0],
            loads=list(small),
            late_loads=("features", "waves", "unwaves"),
            stores=list(kept),
        )
        dma = pltpu.SemaphoreType.DMA
        scratch = {}

        def hold(**held):
            for name, kind in held.items():
                scratch[name] = pltpu.VMEM(*kind)

        for name, value in small.items():
            scratch[name] = pltpu.VMEM(value.shape, value.dtype)
        for name, kind in kept.items():
            scratch[name] = pltpu.VMEM(*kind)
        hold(x_in=((rows, D), BF16))
        hold(unit=((rows, D), F32))
        hold(scale=((rows, LANES), F32))
        hold(par_own=((8, WIDE), F32))
        hold(par_in=((8, WIDE), F32))
        hold(par_grad=((8, WIDE), F32))
        hold(taps=((8, WIDE), F32))
        hold(win=((3 * channels, D), BF16))
        hold(win_apart=((WIDE, D), BF16))
        hold(wout=((LANES, D), BF16))
        hold(wup=((D, hidden), BF16))
        hold(wdn=((hidden, D), BF16))
        hold(order=((3 * channels, WIDE), BF16))
        hold(order_wide=((3 * channels, WIDE), F32))
        hold(first=((FILT, LONG), F32))
        hold(first_sum=((FILT, LONG), F32))
        hold(first_cos=((FILT, LONG), F32))
        hold(second=((FILT, LONG), F32))
        hold(second_sum=((FILT, LONG), F32))
        hold(second_cos=((FILT, LONG), F32))
        hold(own_filter=((FILT, LANES), F32))
        hold(own_decay=((8, LANES), F32))
        hold(kernel=((LONG, LANES), F32))
        hold(raw_grad=((LONG, LANES), F32))
        hold(spread=((BINS, COUNT * LANES), BF16))
        hold(kernel_wave=((BINS, COUNT * LANES), F32))
        hold(signal_wave=((BINS, COUNT * LANES), F32))
        hold(grad_wave=((BINS, COUNT * LANES), F32))
        hold(product=((BINS, COUNT * LANES), BF16))
        hold(back_product=((2 * BINS, COUNT * LANES), BF16))
        hold(g_one=((LONG, D), BF16))
        hold(g_out=((LONG, D), BF16))
        hold(g_two=((LONG, D), BF16))
        hold(g_back=((LONG, D), BF16))
        hold(projected=((LONG, WIDE), F32))
        hold(short=((LONG, WIDE), F32))
        hold(short_grad=((LONG, WIDE), F32))
        hold(signal=((BLOCK, COUNT * LANES), BF16))
        hold(direct_low=((BLOCK, COUNT * LANES), BF16))
        hold(direct=((LONG, LANES), F32))
        hold(mixed=((LONG, LANES), BF16))
        hold(middle=((rows, D), F32))
        hold(middle_grad=((rows, D), F32))
        hold(input_grad=((rows, D), BF16))
        hold(block_out=((rows, D), BF16))
        hold(active=((LONG, hidden), BF16))
        hold(hidden_grad=((LONG, hidden), BF16))
        hold(projected_grad=((LONG, 3 * channels), BF16))
        hold(chip_out=((4, LONG // 2, D), BF16))
        hold(chip_in=((4, LONG // 2, D), BF16))
        hold(link_out=((4, LONG // 2, D), BF16))
        hold(link_in=((4, LONG // 2, D), BF16))
        for name, full in dict(
            _in=(in_rows, D), _out=(LANES, D), _up=(D, hidden), _dn=(down_rows, D)
        ).items():
            part = (full[0] // ranks, full[1])
            for kind, shape in dict(grad=full, part=part, y=(ranks,) + part, z=part).items():
                scratch[kind + name] = pltpu.VMEM(shape, BF16)
        hold(pay=((PAY_ROWS, LANES), F32))
        hold(pay_in=((PAY_ROWS // 2, LANES), F32))
        hold(pay_sum=((PAY_ROWS // 2, LANES), F32))
        hold(pay_held=((halves, PAY_ROWS // group, LANES), F32))
        hold(pay_cross=((2 * ranks, PAY_ROWS // group, LANES), F32))
        hold(late=((8, LANES), F32))
        hold(late_in=((8, LANES), F32))
        hold(late_held=((halves, 8, LANES), F32))
        hold(late_cross=((2 * ranks, 8, LANES), F32))
        hold(shard_y=((ranks, SHARD_ROWS, LANES), F32))
        hold(shard_q=((2, SHARD_ROWS, LANES), F32))
        for name, shape in dict(
            take=(7,),
            give=(2,),
            cut=(7, ranks),
            gather=(6, halves),
            hop=(6, halves),
            chip=(4, LONG // 2 // BLOCK),
            link=(4, halves),
            y=(4, ranks),
            z=(4,),
            out=(4, ranks),
            fin=(4, ranks),
            pay=(1,),
            paylink=(halves,),
            late=(halves,),
            sy=(ranks,),
            sq=(1,),
            cross=(2, 2 * ranks),
        ).items():
            scratch[name + "_send"] = dma(shape)
            scratch[name + "_recv"] = dma(shape)
        scratch["take_local"] = dma((7,))
        scratch["give_local"] = dma((2,))
        scratch["load_sem"] = dma((len(small),))
        scratch["store_sem"] = dma((len(kept),))
        names = list(inputs) + list(outputs) + list(scratch)
        results = pl.pallas_call(
            functools.partial(fused, sizes, names),
            out_shape=[jax.ShapeDtypeStruct(*kind) for kind in outputs.values()],
            in_specs=[i[1] for i in inputs.values()],
            out_specs=[anywhere for _ in outputs],
            scratch_shapes=list(scratch.values()),
            compiler_params=pltpu.CompilerParams(
                collective_id=0,
                has_side_effects=True,
                vmem_limit_bytes=60 * 2**20,
            ),
            name="block",
        )(*[i[0] for i in inputs.values()])
        finals = dict(
            gwin_wide=(3 * channels, D),
            gwout_wide=(channels, D),
            gwup_wide=(D, hidden),
            gwdn_wide=(hidden, D),
            input_wide=(rows, D),
            mixer_gain=(D,),
            in_bias=(3 * channels,),
            short_taps=(3, 3 * channels),
            skip_gain=(channels,),
            out_bias=(D,),
            ffn_gain=(D,),
            up_bias=(hidden,),
            down_bias=(D,),
            embed_weight=(EMB, FILT),
            embed_bias=(FILT,),
            embed_freq=(FILT,),
            hidden_weight=(FILT, FILT),
            hidden_bias=(FILT,),
            hidden_freq=(FILT,),
            filter_weight=(FILT, D),
            decay_rate=(D,),
        )
        loads = ["block", "input"] + list(kept)
        closing = types.SimpleNamespace(
            halves=halves, channels=channels, hidden=hidden, loads=loads, stores=list(finals)
        )
        scratch = dict(
            block=pltpu.VMEM((rows, D), BF16),
            input=pltpu.VMEM((rows, D), BF16),
            decay_row=pltpu.VMEM((8, D), F32),
        )
        for name, kind in kept.items():
            scratch[name] = pltpu.VMEM(*kind)
        for name, shape in finals.items():
            scratch[name] = pltpu.VMEM(shape, F32)
        scratch["load_sem"] = dma((len(loads),))
        scratch["store_sem"] = dma((len(finals),))
        scratch["block_sem"] = dma
        names = [name + "_any" for name in loads] + ["block_out"]
        names += [name + "_out" for name in finals] + ["penalty_out"] + list(scratch)
        done = pl.pallas_call(
            functools.partial(close, closing, names),
            out_shape=[jax.ShapeDtypeStruct((rows, D), BF16)]
            + [jax.ShapeDtypeStruct(shape, F32) for shape in finals.values()]
            + [jax.ShapeDtypeStruct((1,), F32)],
            in_specs=[anywhere] * len(loads),
            out_specs=[anywhere] * (1 + len(finals)) + [scalar],
            scratch_shapes=list(scratch.values()),
            compiler_params=pltpu.CompilerParams(vmem_limit_bytes=60 * 2**20),
            name="close",
        )(*results)
        out = types.SimpleNamespace(**dict(zip(finals, done[1:-1])))
        return (
            done[0],
            out.input_wide,
            done[-1].reshape(()),
            out.mixer_gain,
            out.gwin_wide.T,
            out.in_bias,
            out.short_taps,
            out.skip_gain,
            out.gwout_wide,
            out.out_bias,
            out.ffn_gain,
            out.gwup_wide,
            out.up_bias,
            out.gwdn_wide,
            out.down_bias,
            out.embed_weight,
            out.embed_bias,
            out.embed_freq,
            out.hidden_weight,
            out.hidden_bias,
            out.hidden_freq,
            out.filter_weight,
            out.decay_rate,
        )

    placed = (
        P(("dp", "mp"), None),
        P(),
        P(None, "mp"),
        P("mp"),
        P(None, "mp"),
        P("mp"),
        P("mp", None),
        P(),
        P(),
        P(None, "mp"),
        P("mp"),
        P("mp", None),
        P(),
        P(),
        P(),
        P(),
        P(),
        P(),
        P(),
        P(),
        P(),
        P(("dp", "mp"), None),
        P(),
        P(),
        P(),
    )
    return jax.shard_map(
        per_device,
        mesh=mesh,
        in_specs=placed,
        out_specs=(
            P(("dp", "mp"), None),
            P(("dp", "mp"), None),
            P(),
            P(),
            P(None, "mp"),
            P("mp"),
            P(None, "mp"),
            P("mp"),
            P("mp", None),
            P(),
            P(),
            P(None, "mp"),
            P("mp"),
            P("mp", None),
            P(),
            P(),
            P(),
            P(),
            P(),
            P(),
            P(),
            P(),
            P(),
        ),
        check_vma=False,
    )
```

time: 212 us -> 144 us (0.68)
  Pallas kernels: 179 us -> 143 us
  local copies, waits for them, and re-layouts: 26.5 us -> 0 us
  other arithmetic: 4.2 us -> 0 us
    pallas_call x1, Pallas kernels: 179 us -> 139 us  [per_device(): pl.pallas_call(functools.partial(fused, sizes, names), out_shape=[jax.Sha...]
    reshape x9 -> x0, local copies, waits for them, and re-layouts: 11 us -> none  [the longest x7 8.82 us: per_device(): row = lambda value: value.reshape(1, -1)]
    slice x7 -> x0, local copies, waits for them, and re-layouts: 7.66 us -> none  [the longest x1 1.69 us: vector_of(): return pay[PAY_HID:PAY_HID + FILT, FILT + k]]
    unnamed x18 -> x0, local copies, waits for them, and re-layouts: 4.81 us -> none
    pallas_call x0 -> x1, Pallas kernels: none -> 4.16 us  [per_device(): pl.pallas_call(functools.partial(close, closing, names), out_shape=[jax.S...]
    convert_element_type x3 -> x0, other arithmetic: 2.92 us -> none  [the longest x1 1.09 us: per_device(): out['gwdn'][0:hidden].astype(F32)]
where the time goes in v3:
time: 144 us
  Pallas kernels  143 us (99%)
    pallas_call x1, Pallas kernels, per_device(): pl.pallas_call(functools.partial(fused, sizes, names), out_shape=[jax.Sha...  139 us
    pallas_call x1, Pallas kernels, per_device(): pl.pallas_call(functools.partial(close, closing, names), out_shape=[jax.S...  4.16 us

profile of v3, /device:TPU:0, one launch (start us, length us, event | category | flops | bytes accessed | tf_op | source)
XLA Modules:
  0.0 143.6 jit_solution(7216350635353413695)
XLA Ops:
  0.7 138.6 %block.1 = (bf16[128,768]{1,0:T(8,128)(2,1)}, bf16[128,768]{1,0:T(8,128)(2,1)}, bf16[288,768]{1,0:T(8,128)(2,1)}, bf16[128,768]{1,0:T(8,128)(2,1)}, bf16[768,384...) custom-call(bf16[128,768]{1,0:T(8,128)(2,1)} %refs_0_.1, ...), custom_call_target="tpu_custom_call" | custom-call | tf_op jit(solution)/shard_map/block/pallas_call | solution.py:1423
  139.2 4.2 %close.1 = (bf16[128,768]{1,0:T(8,128)(2,1)}, f32[288,768]{1,0:T(8,128)}, f32[96,768]{1,0:T(8,128)}, f32[768,384]{1,0:T(8,128)}, f32[384,768]{1,0:T(8,128)}, /*i...) custom-call(bf16[128,768]{1,0:T(8,128)(2,1)} %get-tuple-element.57.r, ...), custom_call_target="tpu_custom_call" | custom-call | tf_op jit(solution)/shard_map/close/pallas_call | solution.py:1477

commit v4 on v3

--- a/solution.py
+++ b/solution.py
@@ -27,7 +27,7 @@
 ROOT = math.sqrt(2.0 / math.pi)
 CUBE = 0.044715
 
-PAY_VEC, PAY_PEN, PAY_HID, PAY_EMB, PAY_ROWS = 0, 18, 24, 88, 128
+PAY_VEC, PAY_HID, PAY_EMB, PAY_PEN, PAY_ROWS = 0, 24, 88, 121, 128
 SHARD_DECAY, SHARD_PAR, SHARD_ROWS = 64, 72, 96
 
 
@@ -618,26 +618,37 @@
         grad = (slope * dot_nt(r.g_out[at, :], r.wdn[...])).astype(BF16)
         r.active[at, :] = active
         r.hidden_grad[at, :] = grad
-        return dot_nt(grad, r.wup[...]), dot(active, r.wdn[...])
+        return dot_nt(grad, r.wup[...])
 
     def feed_step(i, carry):
         t, own = i // 2, i % 2
-        back, forth = feed(half_chunk(own * c + (1 - own) * other, t))
+        back = feed(half_chunk(own * c + (1 - own) * other, t))
 
         @pl.when(own == 0)
         def _():
             chip_give(1, t, back)
-            chip_give(2, t, forth)
 
         @pl.when(own == 1)
         def _():
             chip_add(1, t, back)
             link_start(1, t)
-            chip_add(2, t, forth)
 
         return carry
 
     lax.fori_loop(0, 2 * chunks, feed_step, 0)
+
+    def down(at):
+        return dot(r.active[at, :], r.wdn[...])
+
+    def down_give(t, carry):
+        chip_give(2, t, down(half_chunk(other, t)))
+        return carry
+
+    def down_add(t, carry):
+        chip_add(2, t, down(half_chunk(c, t)))
+        return carry
+
+    lax.fori_loop(0, chunks, down_give, 0)
 
     sums = [
         (r.grad_in, r.part_in, r.y_in, r.z_in, r.gwin),
@@ -764,6 +775,7 @@
     sum_start(3)
     weight_grad(r.grad_up, r.g_two, r.hidden_grad)
     sum_start(2)
+    lax.fori_loop(0, chunks, down_add, 0)
 
     seed = r.g_out[mine, :].astype(F32)
     ffn_back = scatter_finish(1)
@@ -865,7 +877,16 @@
         par_grad[t + 1 : t + 2, :] = tap_totals[t]
 
     sum_cross(1)
-    scatter(3, lambda at: dot(r.projected_grad[at, :], r.win[...]))
+
+    r.gain_sum[...] = jnp.zeros_like(r.gain_sum)
+
+    def normed_back(at):
+        value = dot(r.projected_grad[at, :], r.win[...])
+        weighed = value * r.g_one[at, :].astype(F32)
+        r.gain_sum[...] += jnp.sum(jnp.reshape(weighed, (BLOCK // 8, 8, D)), axis=0)
+        return value
+
+    scatter(3, normed_back)
 
     weight_grad(r.grad_in, r.projected_grad, r.g_one, True)
     sum_start(0)
@@ -910,6 +931,10 @@
     for dy in range(1, ranks):
         shard_y(dy).start()
     r.pay[PAY_PEN : PAY_PEN + 1, :] = penalty
+    gain_row = jnp.sum(r.gain_sum[...], axis=0, keepdims=True) / line(r.mixer_gain)
+    for k in range(D // LANES):
+        at = PAY_VEC + 3 * (D // LANES) + k
+        r.pay[at : at + 1, :] = gain_row[:, k * LANES : (k + 1) * LANES]
     second_grad = dot_nt(own_filter, r.raw_grad[...], HIGH)
     angle_grad = second_grad * r.second_cos[...]
     freq_grad = jnp.sum(angle_grad * r.second_sum[...], axis=1, keepdims=True)
@@ -1046,28 +1071,6 @@
         r.middle_grad[...] + norm_back(mixer_back, line(r.mixer_gain), unit, scale)
     ).astype(BF16)
     give_start(0)
-    gain_row = jnp.sum(mixer_back * unit, axis=0, keepdims=True)
-    r.late[...] = jnp.zeros_like(r.late)
-    for k in range(D // LANES):
-        r.late[k : k + 1, :] = gain_row[:, k * LANES : (k + 1) * LANES]
-
-    def late_chip():
-        return remote(r.late, r.late_in, r.late_send.at[0], r.late_recv.at[0], sibling)
-
-    def late_links():
-        return [
-            remote(
-                r.late_held.at[j],
-                r.late_held.at[j],
-                r.late_send.at[k],
-                r.late_recv.at[k],
-                device(y, c, q, ahead(k)),
-            )
-            for k in range(1, halves)
-        ]
-
-    late_chip().start()
-
     def store(name):
         i = s.stores.index(name)
         return pltpu.make_async_copy(
@@ -1076,20 +1079,7 @@
 
     r.pay_total[seat(5, c, j), :] = slots_sum(0, r.pay_cross)
     gather_start(5, r.pay_total)
-    late_chip().wait_recv()
-    r.late_held[j] = r.late[...] + r.late_in[...]
-    for copy in late_links():
-        copy.start()
     sum_close(0)
-    for k in range(1, halves):
-        came = r.late_held.at[behind(k)]
-        remote(
-            came, came, r.late_send.at[k], r.late_recv.at[k], device(y, c, q, behind(k))
-        ).wait_recv()
-    r.late_cross[slot] = added(r.late_held, halves)
-    for copy in slots_copies(1, r.late_cross):
-        copy.start()
-
     gather_finish(4, r.shards)
     store("shards").start()
     home = pl.multiple_of((q * halves + j) * SHARD_ROWS, SHARD_ROWS)
@@ -1105,8 +1095,6 @@
         store(name).start()
     gather_finish(5, r.pay_total)
     store("pay_total").start()
-    r.late_total[...] = slots_sum(1, r.late_cross)
-    store("late_total").start()
     sum_finish(0)
     store("gwin").start()
     for name in s.stores:
@@ -1118,8 +1106,7 @@
     for dy in range(1, ranks):
         shard_y(dy).wait_send()
     shard_q().wait_send()
-    late_chip().wait_send()
-    for copy in late_links() + slots_copies(0, r.pay_cross) + slots_copies(1, r.late_cross):
+    for copy in slots_copies(0, r.pay_cross):
         copy.wait_send()
 
     @pl.when(moved)
@@ -1189,8 +1176,7 @@
     put(hidden_bias=vector_of(1))
     put(hidden_freq=vector_of(0))
     r.penalty_out[0] = jnp.sum(pay[PAY_PEN : PAY_PEN + 1, :])
-    load("late_total").wait()
-    put(mixer_gain=long_row(r.late_total, 0))
+    put(mixer_gain=long_row(pay, PAY_VEC + 3 * lines))
     load("par_wide").wait()
     load("par_close").wait()
     put(in_bias=r.par_close[0:1, :])
@@ -1294,7 +1280,6 @@
             gwup=((D, hidden), BF16),
             gwdn=((down_rows, D), BF16),
             pay_total=((PAY_ROWS, LANES), F32),
-            late_total=((8, LANES), F32),
             shards=((group * SHARD_ROWS, LANES), F32),
             par_wide=((8, WIDE), F32),
             par_close=((8, 3 * channels), F32),
@@ -1383,15 +1368,12 @@
             part = (full[0] // ranks, full[1])
             for kind, shape in dict(grad=full, part=part, y=(ranks,) + part, z=part).items():
                 scratch[kind + name] = pltpu.VMEM(shape, BF16)
+        hold(gain_sum=((8, D), F32))
         hold(pay=((PAY_ROWS, LANES), F32))
         hold(pay_in=((PAY_ROWS // 2, LANES), F32))
         hold(pay_sum=((PAY_ROWS // 2, LANES), F32))
         hold(pay_held=((halves, PAY_ROWS // group, LANES), F32))
         hold(pay_cross=((2 * ranks, PAY_ROWS // group, LANES), F32))
-        hold(late=((8, LANES), F32))
-        hold(late_in=((8, LANES), F32))
-        hold(late_held=((halves, 8, LANES), F32))
-        hold(late_cross=((2 * ranks, 8, LANES), F32))
         hold(shard_y=((ranks, SHARD_ROWS, LANES), F32))
         hold(shard_q=((2, SHARD_ROWS, LANES), F32))
         for name, shape in dict(
@@ -1408,7 +1390,6 @@
             fin=(4, ranks),
             pay=(1,),
             paylink=(halves,),
-            late=(halves,),
             sy=(ranks,),
             sq=(1,),
             cross=(2, 2 * ranks),

time: 144 us -> 140 us (0.972)
  Pallas kernels: 143 us -> 139 us
    pallas_call x1, Pallas kernels: 139 us -> 135 us  [per_device(): pl.pallas_call(functools.partial(fused, sizes, names), out_shape=[jax.Sha...]
where the time goes in v4:
time: 140 us
  Pallas kernels  139 us (99%)
    pallas_call x1, Pallas kernels, per_device(): pl.pallas_call(functools.partial(fused, sizes, names), out_shape=[jax.Sha...  135 us
    pallas_call x1, Pallas kernels, per_device(): pl.pallas_call(functools.partial(close, closing, names), out_shape=[jax.S...  4.15 us

profile of v4, /device:TPU:0, one launch (start us, length us, event | category | flops | bytes accessed | tf_op | source)
XLA Modules:
  0.0 140.1 jit_solution(462012506426707361)
XLA Ops:
  0.7 135.1 %block.1 = (bf16[128,768]{1,0:T(8,128)(2,1)}, bf16[128,768]{1,0:T(8,128)(2,1)}, bf16[288,768]{1,0:T(8,128)(2,1)}, bf16[128,768]{1,0:T(8,128)(2,1)}, bf16[768,384...) custom-call(bf16[128,768]{1,0:T(8,128)(2,1)} %refs_0_.1, ...), custom_call_target="tpu_custom_call" | custom-call | tf_op jit(solution)/shard_map/block/pallas_call | solution.py:1404
  135.8 4.2 %close.1 = (bf16[128,768]{1,0:T(8,128)(2,1)}, f32[288,768]{1,0:T(8,128)}, f32[96,768]{1,0:T(8,128)}, f32[768,384]{1,0:T(8,128)}, f32[384,768]{1,0:T(8,128)}, /*i...) custom-call(bf16[128,768]{1,0:T(8,128)(2,1)} %get-tuple-element.56.r, ...), custom_call_target="tpu_custom_call" | custom-call | tf_op jit(solution)/shard_map/close/pallas_call | solution.py:1458

commit v5 on v4

--- a/solution.py
+++ b/solution.py
@@ -758,12 +758,13 @@
             y_copy(w, dy).wait_send()
 
     def weight_grad(target, left, right, by_right=False):
+        if by_right:
+            target[0 : left.shape[1], :] = dot_tn(left[...], right[...]).astype(BF16)
+            return
+
         def chunk(i, carry):
             at = pl.ds(pl.multiple_of(i * BLOCK, BLOCK), BLOCK)
-            if by_right:
-                target[0 : left.shape[1], at] = dot_tn(left[...], right[:, at]).astype(BF16)
-            else:
-                target[at, :] = dot_tn(left[:, at], right[...]).astype(BF16)
+            target[at, :] = dot_tn(left[:, at], right[...]).astype(BF16)
             return carry
 
         lax.fori_loop(0, D // BLOCK, chunk, 0)

time: 140 us -> 139 us (level)
  no operation moved by 1% of the time
where the time goes in v5:
time: 139 us
  Pallas kernels  138 us (99%)
    pallas_call x1, Pallas kernels, per_device(): pl.pallas_call(functools.partial(fused, sizes, names), out_shape=[jax.Sha...  134 us
    pallas_call x1, Pallas kernels, per_device(): pl.pallas_call(functools.partial(close, closing, names), out_shape=[jax.S...  4.15 us

profile of v5, /device:TPU:0, one launch (start us, length us, event | category | flops | bytes accessed | tf_op | source)
XLA Modules:
  0.0 139.2 jit_solution(10989830340140125468)
XLA Ops:
  0.7 134.2 %block.1 = (bf16[128,768]{1,0:T(8,128)(2,1)}, bf16[128,768]{1,0:T(8,128)(2,1)}, bf16[288,768]{1,0:T(8,128)(2,1)}, bf16[128,768]{1,0:T(8,128)(2,1)}, bf16[768,384...) custom-call(bf16[128,768]{1,0:T(8,128)(2,1)} %refs_0_.1, ...), custom_call_target="tpu_custom_call" | custom-call | tf_op jit(solution)/shard_map/block/pallas_call | solution.py:1405
  134.9 4.2 %close.1 = (bf16[128,768]{1,0:T(8,128)(2,1)}, f32[288,768]{1,0:T(8,128)}, f32[96,768]{1,0:T(8,128)}, f32[768,384]{1,0:T(8,128)}, f32[384,768]{1,0:T(8,128)}, /*i...) custom-call(bf16[128,768]{1,0:T(8,128)(2,1)} %get-tuple-element.56.r, ...), custom_call_target="tpu_custom_call" | custom-call | tf_op jit(solution)/shard_map/close/pallas_call | solution.py:1459
